TPU v7x, 128 devices: a whole 4x4x4 slice. The times are simulated.
128 devices in a mesh: dp: 32 (over x, z, core), tp: 4 (over y).
Axes of the slice: x: 4, y: 4, z: 4, core: 2. Of those that a mesh axis runs over, the one named last changes fastest.
Arguments:
- hidden_in: bfloat16 [8192, 7168], P('dp', 'tp'), may hold values from -6 to 6
- lengths: int32 [32], P('dp'), may hold values from 1 to 256, 4096 in all
- routes: int32 [8192, 8], P('dp'), may hold values from 0 to 255, all different within a row; in each aligned block of 256 rows (0 to 255, 256 to 511, ...) at most 12 rows name the same one
- route_weights: float32 [8192, 8], P('dp'), may hold values from 0.1 to 1
- placement: int32 [32], replicated, may hold values from 0 to 31, each once
- shared_gate: bfloat16 [7168, 1024], P(None, 'tp'), may hold values from -0.0625 to 0.0625
- shared_up: bfloat16 [7168, 1024], P(None, 'tp'), may hold values from -0.0625 to 0.0625
- shared_down: bfloat16 [1024, 7168], P('tp'), may hold values from -0.1875 to 0.1875
- expert_gate: bfloat16 [32, 7168, 1024], P('dp', None, 'tp'), may hold values from -0.0625 to 0.0625
- expert_up: bfloat16 [32, 7168, 1024], P('dp', None, 'tp'), may hold values from -0.0625 to 0.0625
- expert_down: bfloat16 [32, 1024, 7168], P('dp', 'tp'), may hold values from -0.1875 to 0.1875
Outputs:
- moe_out: bfloat16 [8192, 7168], P('dp', 'tp')
Inputs may be any that keep to these rules, and one draw needn't show every extreme that they name: `lengths`: one length for each request; they sum to 4096 and the largest is exactly 256. `routes`: each row names 8 different experts; among the 256 rows of one request no expert is named by more than 12 rows, a bound that some block reaches. `placement`: each slot of 0 to 31 holds exactly one expert.
All inputs are finite; a program needn't handle non-finite values. No bound on the sum of `lengths` on one device may be relied on, other than what follows from the above.
Results may differ from a plain program's by a relative error of at most 0.005.
Values may be sent and summed in bfloat16 or wider, within the bound.
A program may use at most 256 MiB of HBM per device.

v0:
```python
import jax
import jax.numpy as jnp
from jax import lax
from jax.sharding import PartitionSpec as P

MOST_R = 12


def gated_hidden(gate_total, up_total):
    return (jax.nn.silu(gate_total) * up_total).astype(jnp.bfloat16)


def weighted_pick(returned_rows, target, route_weights):
    live_route = target >= 0
    safe_index = jnp.where(live_route, target, 0)
    factors = jnp.where(live_route, route_weights, 0.0)
    total = jnp.zeros((target.shape[0], returned_rows.shape[1]), jnp.float32)
    for route in range(target.shape[1]):
        total = total + factors[:, route][:, None] * returned_rows[safe_index[:, route]]
    return total


def local(
    hidden_in,
    lengths,
    routes,
    route_weights,
    placement,
    shared_gate,
    shared_up,
    shared_down,
    expert_gate,
    expert_up,
    expert_down,
):
    rank_rows = hidden_in.shape[0]
    quarter = hidden_in.shape[1]
    groups = lax.axis_size("dp")
    slices = lax.axis_size("tp")
    full_width = quarter * slices
    window = placement.shape[0]
    per_peer = MOST_R
    slot_count = groups * per_peer
    is_live = jnp.arange(rank_rows, dtype=jnp.int32) < lengths[0]
    shard_cols = lax.all_gather(hidden_in, "tp", axis=1, tiled=True)
    gate_rows = shared_gate
    up_rows = shared_up
    shared_gate_sum = jnp.dot(shard_cols, gate_rows, preferred_element_type=jnp.float32)
    shared_up_sum = jnp.dot(shard_cols, up_rows, preferred_element_type=jnp.float32)
    shared_part = jnp.dot(
        gated_hidden(shared_gate_sum, shared_up_sum),
        shared_down,
        preferred_element_type=jnp.float32,
    )
    in_window = (routes < window) & is_live[:, None]
    expert_ids = jnp.where(in_window, routes, 0)
    matches = (
        expert_ids[:, :, None] == jnp.arange(window, dtype=jnp.int32)[None, None, :]
    ) & in_window[:, :, None]
    hit_counts = matches.astype(jnp.int32)
    per_row = jnp.sum(hit_counts, axis=1)
    earlier = jnp.cumsum(per_row, axis=0) - per_row
    position = jnp.sum(hit_counts * earlier[:, None, :], axis=2)
    holder = jnp.sum(hit_counts * placement[None, None, :], axis=2)
    target = jnp.where(in_window, holder * per_peer + position, -1)
    picked = target[:, :, None] == jnp.arange(slot_count, dtype=jnp.int32)[None, None, :]
    selector = jnp.any(picked, axis=1).astype(jnp.bfloat16)
    outgoing = jnp.einsum(
        "cs,cq->sq", selector, hidden_in, preferred_element_type=jnp.float32
    ).astype(jnp.bfloat16)
    arrived = lax.all_to_all(
        outgoing.reshape(groups, per_peer, quarter), "dp", split_axis=0, concat_axis=0, tiled=True
    )
    shard_cols = lax.all_gather(arrived.reshape(slot_count, quarter), "tp", axis=1, tiled=True)
    gate_rows = expert_gate[0]
    up_rows = expert_up[0]
    expert_gate_sum = jnp.dot(shard_cols, gate_rows, preferred_element_type=jnp.float32)
    expert_up_sum = jnp.dot(shard_cols, up_rows, preferred_element_type=jnp.float32)
    expert_part = jnp.dot(
        gated_hidden(expert_gate_sum, expert_up_sum),
        expert_down[0],
        preferred_element_type=jnp.float32,
    )
    came_back = lax.all_to_all(
        expert_part.reshape(groups, per_peer, full_width),
        "dp",
        split_axis=0,
        concat_axis=0,
        tiled=True,
    )
    summands = shared_part + weighted_pick(
        came_back.reshape(slot_count, full_width), target, route_weights
    )
    combined = lax.psum_scatter(summands, "tp", scatter_dimension=1, tiled=True)
    return jnp.where(is_live[:, None], combined, 0.0).astype(jnp.bfloat16)


def solution(mesh):
    in_specs = (
        P("dp", "tp"),
        P("dp"),
        P("dp", None),
        P("dp", None),
        P(),
        P(None, "tp"),
        P(None, "tp"),
        P("tp", None),
        P("dp", None, "tp"),
        P("dp", None, "tp"),
        P("dp", "tp", None),
    )
    out_specs = P("dp", "tp")
    return jax.shard_map(local, mesh=mesh, in_specs=in_specs, out_specs=out_specs, check_vma=False)
```

profile of v0, /device:TPU:1, one launch (start us, length us, event | category | flops | bytes accessed | tf_op | source)
XLA Modules:
  0.0 608.0 jit_solution(10978551063936282849)
XLA Ops:
  10.5 1.6 fusion.6
  12.2 1.8 convolution_convert_fusion
  14.3 35.1 %all_to_all.10 = bf16[32,12,1792]{2,1,0:T(8,128)(2,1)} all-to-all(bf16[32,12,1792]{2,1,0:T(8,128)(2,1)S(1)} %reshape.32), channel_id=1, replica_groups=mesh['dp'=32,'tp'=4] {'dp'}, dimensions={0} | all-to-all | bytes 2752512 | tf_op jit(solution)/shard_map/all_to_all | solution.py:71
  49.4 3.4 reshape.33
  52.8 56.9 %all-gather.5.cloned.1.call-done = bf16[384,7168]{1,0:T(8,128)(2,1)} async-done(((bf16[384,1792]{1,0:T(8,128)(2,1)}), bf16[384,7168]{1,0:T(8,128)(2,1)}) %all-gather.5.cloned.1.call-update) | async-done | bytes 5505040 | tf_op jit(solution)/shard_map/all_gather | solution.py:74
  109.7 5.4 fusion.4
  117.7 7.8 %fusion = f32[32,12,7168]{2,0,1:T(8,128)} fusion(bf16[1,256,7168]{2,1,0:T(8,128)(2,1)} %param.21, bf16[32,12,256]{2,1,0:T(8,128)(2,1)S(1)} %dot_general.29), kind=kOutput, calls=%fused_computation.9 | convolution fusion | flops 1409286144 | bytes 14876672 | tf_op jit(solution)/shard_map/dot_general | solution.py:79
  125.5 15.9 %copy.36 = f32[32,12,7168]{2,1,0:T(8,128)} copy(f32[32,12,7168]{2,0,1:T(8,128)} %fusion) | data formatting | bytes 22020096 | tf_op jit(solution)/shard_map/dot_general | solution.py:79
  141.4 7.7 %all-to-all-start.1 = ((f32[32,12,7168]{2,1,0:T(8,128)}), f32[32,12,7168]{2,1,0:T(8,128)}, u32[]{:S(2)}, u32[]{:S(2)}) async-start(f32[32,12,7168]{2,1,0:T(8,128)} %copy.36), calls=%async_computation.1 | async-start | bytes 29360128 | tf_op jit(solution)/shard_map/all_to_all | solution.py:84
  150.7 45.1 %all-gather.3.cloned.1.call-done = bf16[256,7168]{1,0:T(8,128)(2,1)} async-done(((bf16[256,1792]{1,0:T(8,128)(2,1)}), bf16[256,7168]{1,0:T(8,128)(2,1)}) %all-gather.3.cloned.1.call-update) | async-done | bytes 3670032 | tf_op jit(solution)/shard_map/all_gather | solution.py:45
  195.8 5.0 fusion.25
  200.8 150.4 %all-to-all-done.1 = f32[32,12,7168]{2,1,0:T(8,128)} async-done(((f32[32,12,7168]{2,1,0:T(8,128)}), f32[32,12,7168]{2,1,0:T(8,128)}, u32[]{:S(2)}, u32[]{:S(2)}) %all-to-all-start.1) | async-done | bytes 11010080 | tf_op jit(solution)/shard_map/all_to_all | solution.py:84
  351.2 12.0 %reshape.34 = f32[384,7168]{1,0:T(8,128)} reshape(f32[32,12,7168]{2,1,0:T(8,128)} %all-to-all-done.1) | data formatting | bytes 22020096 | tf_op jit(solution)/shard_map/reshape | solution.py:92
  363.3 12.9 %gather_fusion = f32[256,7168]{1,0:T(8,128)} fusion(f32[384,7168]{1,0:T(8,128)} %reshape.34, s32[1024]{0:T(1024)S(1)} %pad_clamp_fusion.7), kind=kCustom, calls=%fused_computation | custom fusion | bytes 14681088 | tf_op jit(solution)/shard_map/gather | solution.py:19
  376.1 13.0 %gather_fusion.1 = f32[256,7168]{1,0:T(8,128)} fusion(f32[384,7168]{1,0:T(8,128)} %reshape.34, s32[1024]{0:T(1024)S(1)} %pad_clamp_fusion.6), kind=kCustom, calls=%fused_computation.1 | custom fusion | bytes 14681088 | tf_op jit(solution)/shard_map/gather | solution.py:19
  389.1 13.2 %gather_fusion.2 = f32[256,7168]{1,0:T(8,128)} fusion(f32[384,7168]{1,0:T(8,128)} %reshape.34, s32[1024]{0:T(1024)S(1)} %pad_clamp_fusion.5), kind=kCustom, calls=%fused_computation.2 | custom fusion | bytes 14681088 | tf_op jit(solution)/shard_map/gather | solution.py:19
  402.3 12.9 %gather_fusion.3 = f32[256,7168]{1,0:T(8,128)} fusion(f32[384,7168]{1,0:T(8,128)} %reshape.34, s32[1024]{0:T(1024)S(1)} %pad_clamp_fusion.4), kind=kCustom, calls=%fused_computation.3 | custom fusion | bytes 14681088 | tf_op jit(solution)/shard_map/gather | solution.py:19
  415.1 13.1 %gather_fusion.4 = f32[256,7168]{1,0:T(8,128)} fusion(f32[384,7168]{1,0:T(8,128)} %reshape.34, s32[1024]{0:T(1024)S(1)} %pad_clamp_fusion.3), kind=kCustom, calls=%fused_computation.4 | custom fusion | bytes 14681088 | tf_op jit(solution)/shard_map/gather | solution.py:19
  428.3 13.0 %gather_fusion.5 = f32[256,7168]{1,0:T(8,128)} fusion(f32[384,7168]{1,0:T(8,128)} %reshape.34, s32[1024]{0:T(1024)S(1)} %pad_clamp_fusion.2), kind=kCustom, calls=%fused_computation.5 | custom fusion | bytes 14681088 | tf_op jit(solution)/shard_map/gather | solution.py:19
  441.3 13.3 %gather_fusion.6 = f32[256,7168]{1,0:T(8,128)} fusion(f32[384,7168]{1,0:T(8,128)} %reshape.34, s32[1024]{0:T(1024)S(1)} %pad_clamp_fusion.1), kind=kCustom, calls=%fused_computation.6 | custom fusion | bytes 14681088 | tf_op jit(solution)/shard_map/gather | solution.py:19
  454.7 13.0 %gather_fusion.7 = f32[256,7168]{1,0:T(8,128)} fusion(f32[384,7168]{1,0:T(8,128)} %reshape.34, s32[1024]{0:T(1024)S(1)} %pad_clamp_fusion), kind=kCustom, calls=%fused_computation.7 | custom fusion | bytes 14681088 | tf_op jit(solution)/shard_map/gather | solution.py:19
  467.7 27.3 %convolution_add_fusion = f32[256,7168]{1,0:T(8,128)} fusion(bf16[256,7168]{1,0:T(8,128)(2,1)} %param.18, f32[256,7168]{1,0:T(8,128)} %gather_fusion.7, f32[256,7168]{1,0:T(8,128)} %gather_fusion.6, f32[256,7168]{1,0:T(8,128)} %gather_fusion.5, f32[256,7168]{1,0:T(8,128)} %gather_fusion.4, f32[256,7168]{1,0:T(8,128)} %gather_fusion.3, ...), kind=kOutput, calls=%fused_computation.8 | convolution fusion | flops 1908801536 | bytes 77340672 | tf_op jit(solution)/shard_map/dot_general | solution.py:50
  495.0 103.8 %reduce-scatter.2.cloned.1.call-done = f32[256,1792]{1,0:T(8,128)} async-done(((f32[256,7168]{1,0:T(8,128)}), f32[256,1792]{1,0:T(8,128)}) %reduce-scatter.2.cloned.1.call-update) | async-done | bytes 1835024 | tf_op jit(solution)/shard_map/reduce_scatter | solution.py:94
  598.8 2.6 select_convert_fusion
  (58 shorter events, 7.7 us)
Async XLA Ops:
  6.5 103.2 %all-gather.5.cloned.1.call-start = ((), (), s32[]{:S(2)}) async-start(), calls=%async_computation.4 | async-start | bytes 6881280 | tf_op jit(solution)/shard_map/all_gather | solution.py:74
  7.2 1.4 copy-start.9
  109.7 5.4 copy-start.11
  109.7 6.3 %copy-start.12 = (bf16[1,7168,256]{2,1,0:T(8,128)(2,1)S(1)}, bf16[1,7168,256]{2,1,0:T(8,128)(2,1)}, u32[]{:S(2)}) copy-start(bf16[1,7168,256]{2,1,0:T(8,128)(2,1)} %param.20) | copy-start | bytes 11010052
  141.4 209.8 %all-to-all-start.1 = ((f32[32,12,7168]{2,1,0:T(8,128)}), f32[32,12,7168]{2,1,0:T(8,128)}, u32[]{:S(2)}, u32[]{:S(2)}) async-start(f32[32,12,7168]{2,1,0:T(8,128)} %copy.36), calls=%async_computation.1 | async-start | bytes 29360128 | tf_op jit(solution)/shard_map/all_to_all | solution.py:84
  149.1 46.7 %all-gather.3.cloned.1.call-start = ((), (), s32[]{:S(2)}) async-start(), calls=%async_computation.3 | async-start | bytes 4587520 | tf_op jit(solution)/shard_map/all_gather | solution.py:45
  149.9 448.9 %reduce-scatter.2.cloned.1.call-start = ((), (), s32[]{:S(2)}) async-start(), calls=%async_computation.5 | async-start | bytes 9175040 | tf_op jit(solution)/shard_map/reduce_scatter | solution.py:94
  454.6 13.0 %copy-start = (f32[256,256]{1,0:T(8,128)S(1)}, f32[256,256]{1,0:T(8,128)}, u32[]{:S(2)}) copy-start(f32[256,256]{1,0:T(8,128)} %fusion.25) | copy-start | bytes 786436
  454.6 13.0 %copy-start.1 = (f32[256,1]{0,1:T(1,128)S(1)}, f32[256,1]{0,1:T(1,128)}, u32[]{:S(2)}) copy-start(f32[256,1]{0,1:T(1,128)} %get-tuple-element.11) | copy-start | bytes 3076
  454.6 13.0 %copy-start.2 = (f32[256,1]{0,1:T(1,128)S(1)}, f32[256,1]{0,1:T(1,128)}, u32[]{:S(2)}) copy-start(f32[256,1]{0,1:T(1,128)} %get-tuple-element.12) | copy-start | bytes 3076
  454.6 13.0 %copy-start.3 = (f32[256,1]{0,1:T(1,128)S(1)}, f32[256,1]{0,1:T(1,128)}, u32[]{:S(2)}) copy-start(f32[256,1]{0,1:T(1,128)} %get-tuple-element.13) | copy-start | bytes 3076
  454.6 13.0 %copy-start.4 = (f32[256,1]{0,1:T(1,128)S(1)}, f32[256,1]{0,1:T(1,128)}, u32[]{:S(2)}) copy-start(f32[256,1]{0,1:T(1,128)} %get-tuple-element.14) | copy-start | bytes 3076
  454.6 13.0 %copy-start.5 = (f32[256,1]{0,1:T(1,128)S(1)}, f32[256,1]{0,1:T(1,128)}, u32[]{:S(2)}) copy-start(f32[256,1]{0,1:T(1,128)} %get-tuple-element.15) | copy-start | bytes 3076
  454.6 13.0 %copy-start.6 = (f32[256,1]{0,1:T(1,128)S(1)}, f32[256,1]{0,1:T(1,128)}, u32[]{:S(2)}) copy-start(f32[256,1]{0,1:T(1,128)} %get-tuple-element.16) | copy-start | bytes 3076
  454.6 13.0 %copy-start.7 = (f32[256,1]{0,1:T(1,128)S(1)}, f32[256,1]{0,1:T(1,128)}, u32[]{:S(2)}) copy-start(f32[256,1]{0,1:T(1,128)} %get-tuple-element.17) | copy-start | bytes 3076
  454.7 13.0 %copy-start.8 = (f32[256,1]{0,1:T(1,128)S(1)}, f32[256,1]{0,1:T(1,128)}, u32[]{:S(2)}) copy-start(f32[256,1]{0,1:T(1,128)} %get-tuple-element.18) | copy-start | bytes 3076
  495.0 103.8 %copy-start.10 = (pred[256]{0:T(512)(128)(4,1)S(1)}, pred[256]{0:T(512)(128)(4,1)}, u32[]{:S(2)}) copy-start(pred[256]{0:T(512)(128)(4,1)} %copy-done.9) | copy-start | bytes 772
Sparse Core Ops, SparseCore 0:
  53.0 56.7 all-gather.4
  151.6 44.1 all-gather.2
  495.1 103.5 reduce-scatter.1
where the time goes:
time: 611 us; the launch traced here: 608 us
  waiting for transfers between devices  357 us (58%)
  local copies, waits for them, and re-layouts  138 us (23%)
  matrix products  48.8 us (8%)
  blocking collectives  35.1 us (6%)
  between operations  14.2 us (2%)
  starting transfers between devices  7.8 us (1%)
  other arithmetic  7.27 us (1%)
    all_to_all x1, waiting for transfers between devices, local(): lax.all_to_all(expert_part.reshape(groups, per_peer, full_width), 'dp', s...  150 us
    gather x8, local copies, waits for them, and re-layouts, weighted_pick(): returned_rows[safe_index[:, route]]  104 us
    reduce_scatter x1, waiting for transfers between devices, local(): combined = lax.psum_scatter(summands, 'tp', scatter_dimension=1, tiled=True)  104 us
    all_gather x1, waiting for transfers between devices, local(): lax.all_gather(arrived.reshape(slot_count, quarter), 'tp', axis=1, tiled=...  56.9 us
    all_gather x1, waiting for transfers between devices, local(): shard_cols = lax.all_gather(hidden_in, 'tp', axis=1, tiled=True)  45.1 us
    all_to_all x1, blocking collectives, local(): lax.all_to_all(outgoing.reshape(groups, per_peer, quarter), 'dp', split_a...  35.1 us
    dot_general x1, matrix products, local(): jnp.dot(gated_hidden(shared_gate_sum, shared_up_sum), shared_down, prefer...  27.3 us
    dot_general x2, local copies, waits for them, and re-layouts, local(): jnp.dot(gated_hidden(expert_gate_sum, expert_up_sum), expert_down[0], pre...  15.9 us
  transfers between devices with their start and end apart: 4, of which 4 were waited for; matrix products, arithmetic and copies ran while one was open for 1% of the time, Pallas kernels for 0%

commit v1 on v0

--- a/solution.py
+++ b/solution.py
@@ -8,16 +8,6 @@
 
 def gated_hidden(gate_total, up_total):
     return (jax.nn.silu(gate_total) * up_total).astype(jnp.bfloat16)
-
-
-def weighted_pick(returned_rows, target, route_weights):
-    live_route = target >= 0
-    safe_index = jnp.where(live_route, target, 0)
-    factors = jnp.where(live_route, route_weights, 0.0)
-    total = jnp.zeros((target.shape[0], returned_rows.shape[1]), jnp.float32)
-    for route in range(target.shape[1]):
-        total = total + factors[:, route][:, None] * returned_rows[safe_index[:, route]]
-    return total
 
 
 def local(
@@ -81,17 +71,29 @@
         expert_down[0],
         preferred_element_type=jnp.float32,
     )
+    rows_back = lax.all_to_all(
+        expert_part.astype(jnp.bfloat16), "tp", split_axis=1, concat_axis=0, tiled=True
+    ).reshape(slices, slot_count, quarter)
+    expert_sum = jnp.sum(rows_back.astype(jnp.float32), axis=0).astype(jnp.bfloat16)
     came_back = lax.all_to_all(
-        expert_part.reshape(groups, per_peer, full_width),
+        expert_sum.reshape(groups, per_peer, quarter),
         "dp",
         split_axis=0,
         concat_axis=0,
         tiled=True,
+    ).reshape(slot_count, quarter)
+    shared_rows = lax.all_to_all(
+        shared_part.astype(jnp.bfloat16), "tp", split_axis=1, concat_axis=0, tiled=True
+    ).reshape(slices, rank_rows, quarter)
+    shared_sum = jnp.sum(shared_rows.astype(jnp.float32), axis=0)
+    weight_of = jnp.sum(jnp.where(picked, route_weights[:, :, None], 0.0), axis=1)
+    coarse = weight_of.astype(jnp.bfloat16)
+    fine = (weight_of - coarse.astype(jnp.float32)).astype(jnp.bfloat16)
+    combined = (
+        shared_sum
+        + jnp.dot(coarse, came_back, preferred_element_type=jnp.float32)
+        + jnp.dot(fine, came_back, preferred_element_type=jnp.float32)
     )
-    summands = shared_part + weighted_pick(
-        came_back.reshape(slot_count, full_width), target, route_weights
-    )
-    combined = lax.psum_scatter(summands, "tp", scatter_dimension=1, tiled=True)
     return jnp.where(is_live[:, None], combined, 0.0).astype(jnp.bfloat16)
 
 

time: 611 us -> 307 us (0.50)
  waiting for transfers between devices: 357 us -> 181 us
  local copies, waits for them, and re-layouts: 138 us -> 14.4 us
  matrix products: 48.8 us -> 28.5 us
  starting transfers between devices: 7.8 us -> 18.7 us
  other arithmetic: 7.27 us -> 14.4 us
    gather x8 -> x0, local copies, waits for them, and re-layouts: 104 us -> none  [weighted_pick(): returned_rows[safe_index[:, route]]]
    reduce_scatter x1 -> x0, waiting for transfers between devices: 104 us -> none  [local(): combined = lax.psum_scatter(summands, 'tp', scatter_dimension=1, tiled=True)]
    all_to_all x1 -> x3, waiting for transfers between devices: 150 us -> 72.8 us  [the longest x1 36.9 us: local(): lax.all_to_all(shared_part.astype(jnp.bfloat16), 'tp', split_axis=1, conc...]
    dot_general x1, matrix products: 27.3 us -> 9.99 us  [local(): jnp.dot(gated_hidden(shared_gate_sum, shared_up_sum), shared_down, prefer...]
    dot_general x2 -> x0, local copies, waits for them, and re-layouts: 15.9 us -> none  [local(): jnp.dot(gated_hidden(expert_gate_sum, expert_up_sum), expert_down[0], pre...]
    all_to_all x1 -> x3, starting transfers between devices: 7.71 us -> 18.7 us  [the longest x1 8.66 us: local(): lax.all_to_all(expert_sum.reshape(groups, per_peer, quarter), 'dp', split...]
    reduce_sum x0 -> x3, other arithmetic: none -> 10.5 us  [the longest x1 4.18 us: local(): jnp.sum(rows_back.astype(jnp.float32), axis=0).astype(jnp.bfloat16)]
    reshape x2 -> x3, local copies, waits for them, and re-layouts: 12 us -> 1.76 us  [the longest x1 1.42 us: local(): expert_sum.reshape(groups, per_peer, quarter)]
  transfers between devices with their start and end apart: 4 -> 5, of which waited for: 4 -> 5; matrix products, arithmetic and copies ran while one was open for 1% -> 14% of each run, Pallas kernels for 0% -> 0%
where the time goes in v1:
time: 307 us; the launch traced here: 306 us
  waiting for transfers between devices  181 us (59%)
  blocking collectives  34.8 us (11%)
  matrix products  28.5 us (9%)
  starting transfers between devices  18.7 us (6%)
  other arithmetic  14.4 us (5%)
  local copies, waits for them, and re-layouts  14.4 us (5%)
  between operations  14.2 us (5%)
    all_gather x1, waiting for transfers between devices, local(): lax.all_gather(arrived.reshape(slot_count, quarter), 'tp', axis=1, tiled=...  56.2 us
    all_gather x1, waiting for transfers between devices, local(): shard_cols = lax.all_gather(hidden_in, 'tp', axis=1, tiled=True)  51.6 us
    all_to_all x1, waiting for transfers between devices, local(): lax.all_to_all(shared_part.astype(jnp.bfloat16), 'tp', split_axis=1, conc...  36.9 us
    all_to_all x1, blocking collectives, local(): lax.all_to_all(outgoing.reshape(groups, per_peer, quarter), 'dp', split_a...  34.8 us
    all_to_all x1, waiting for transfers between devices, local(): lax.all_to_all(expert_sum.reshape(groups, per_peer, quarter), 'dp', split...  19 us
    all_to_all x1, waiting for transfers between devices, local(): lax.all_to_all(expert_part.astype(jnp.bfloat16), 'tp', split_axis=1, conc...  16.9 us
    dot_general x1, matrix products, local(): jnp.dot(gated_hidden(shared_gate_sum, shared_up_sum), shared_down, prefer...  9.99 us
    dot_general x2, matrix products, local(): jnp.dot(shard_cols, gate_rows, preferred_element_type=jnp.float32)  9.65 us
  transfers between devices with their start and end apart: 5, of which 5 were waited for; matrix products, arithmetic and copies ran while one was open for 14% of the time, Pallas kernels for 0%

profile of v1, /device:TPU:1, one launch (start us, length us, event | category | flops | bytes accessed | tf_op | source)
XLA Modules:
  0.0 306.3 jit_solution(6229042243767691143)
XLA Ops:
  9.8 1.6 fusion.5
  11.5 1.8 convolution_convert_fusion.2
  13.6 34.8 %all_to_all.36 = bf16[32,12,1792]{2,1,0:T(8,128)(2,1)} all-to-all(bf16[32,12,1792]{2,1,0:T(8,128)(2,1)S(1)} %reshape.44), channel_id=1, replica_groups=mesh['dp'=32,'tp'=4] {'dp'}, dimensions={0} | all-to-all | bytes 2752512 | tf_op jit(solution)/shard_map/all_to_all | solution.py:61
  48.4 3.4 %reshape.45 = bf16[384,1792]{1,0:T(8,128)(2,1)} reshape(bf16[32,12,1792]{2,1,0:T(8,128)(2,1)} %all_to_all.36) | data formatting | bytes 2752512 | tf_op jit(solution)/shard_map/reshape | solution.py:64
  52.6 56.2 %all-gather.5.cloned.1.call-done = bf16[384,7168]{1,0:T(8,128)(2,1)} async-done(((bf16[384,1792]{1,0:T(8,128)(2,1)}), bf16[384,7168]{1,0:T(8,128)(2,1)}) %all-gather.5.cloned.1.call-update) | async-done | bytes 5505040 | tf_op jit(solution)/shard_map/all_gather | solution.py:64
  108.7 5.4 %fusion.3 = f32[384,256]{1,0:T(8,128)S(1)} fusion(bf16[384,7168]{1,0:T(8,128)(2,1)} %all-gather.5.cloned.1.call-done, bf16[1,7168,256]{2,1,0:T(8,128)(2,1)} %param.19), kind=kOutput, calls=%fused_computation.8 | convolution fusion | flops 1409286144 | bytes 9568256 | tf_op jit(solution)/shard_map/dot_general | solution.py:67
  115.1 1.6 fusion.11
  117.1 1.6 convolution_convert_fusion
  118.7 2.8 copy.46
  121.5 5.3 %all-to-all-start.2 = ((bf16[384,4,1792]{2,0,1:T(8,128)(2,1)}), bf16[384,4,1792]{2,0,1:T(8,128)(2,1)}, u32[]{:S(2)}, u32[]{:S(2)}) async-start(bf16[384,4,1792]{2,0,1:T(8,128)(2,1)} %bitcast.52), calls=%async_computation.2 | async-start | bytes 11010048 | tf_op jit(solution)/shard_map/all_to_all | solution.py:74
  126.8 51.6 %all-gather.3.cloned.1.call-done = bf16[256,7168]{1,0:T(8,128)(2,1)} async-done(((bf16[256,1792]{1,0:T(8,128)(2,1)}), bf16[256,7168]{1,0:T(8,128)(2,1)}) %all-gather.3.cloned.1.call-update) | async-done | bytes 3670032 | tf_op jit(solution)/shard_map/all_gather | solution.py:35
  178.4 4.3 %fusion.26 = f32[256,256]{1,0:T(8,128)S(1)} fusion(bf16[256,7168]{1,0:T(8,128)(2,1)} %all-gather.3.cloned.1.call-done, bf16[7168,256]{1,0:T(8,128)(2,1)} %param.16), kind=kOutput, calls=%fused_computation.46 | convolution fusion | flops 939524096 | bytes 7602176 | tf_op jit(solution)/shard_map/dot_general | solution.py:38
  182.7 10.0 %convolution_convert_fusion.1 = bf16[256,7168]{1,0:T(8,128)(2,1)} fusion(bf16[256,7168]{1,0:T(8,128)(2,1)} %param.18, bf16[256,7168]{1,0:T(8,128)(2,1)} %all-gather.3.cloned.1.call-done, bf16[7168,256]{1,0:T(8,128)(2,1)} %param.17, f32[256,256]{1,0:T(8,128)S(1)} %fusion.26), kind=kOutput, calls=%fused_computation.1 | convolution fusion | flops 1881276416 | bytes 14942208 | tf_op jit(solution)/shard_map/dot_general | solution.py:40
  192.7 4.2 %copy.47 = bf16[32,4,8,1792]{3,2,0,1:T(8,128)(2,1)} copy(bf16[32,4,8,1792]{3,2,1,0:T(8,128)(2,1)} %bitcast.54) | data formatting | bytes 7340032 | tf_op jit(solution)/shard_map/all_to_all | solution.py:85
  196.8 16.9 %all-to-all-done.2 = bf16[384,4,1792]{2,0,1:T(8,128)(2,1)} async-done(((bf16[384,4,1792]{2,0,1:T(8,128)(2,1)}), bf16[384,4,1792]{2,0,1:T(8,128)(2,1)}, u32[]{:S(2)}, u32[]{:S(2)}) %all-to-all-start.2) | async-done | bytes 5505056 | tf_op jit(solution)/shard_map/all_to_all | solution.py:74
  213.8 4.8 %all-to-all-start = ((bf16[256,4,1792]{2,0,1:T(8,128)(2,1)}), bf16[256,4,1792]{2,0,1:T(8,128)(2,1)}, u32[]{:S(2)}, u32[]{:S(2)}) async-start(bf16[256,4,1792]{2,0,1:T(8,128)(2,1)} %bitcast.55), calls=%async_computation | async-start | bytes 7340032 | tf_op jit(solution)/shard_map/all_to_all | solution.py:85
  218.6 4.2 %reduce_sum.62 = bf16[384,1792]{1,0:T(8,128)(2,1)S(1)} reduce(bf16[384,4,1792]{2,0,1:T(8,128)(2,1)} %all-to-all-done.2, bf16[]{:T(256)} %constant.23.clone.1), dimensions={1}, to_apply=%region_8.9 | reduce | flops 2064384 | bytes 6881282 | tf_op jit(solution)/shard_map/reduce_sum | solution.py:77
  224.2 36.9 %all-to-all-done = bf16[256,4,1792]{2,0,1:T(8,128)(2,1)} async-done(((bf16[256,4,1792]{2,0,1:T(8,128)(2,1)}), bf16[256,4,1792]{2,0,1:T(8,128)(2,1)}, u32[]{:S(2)}, u32[]{:S(2)}) %all-to-all-start) | async-done | bytes 3670048 | tf_op jit(solution)/shard_map/all_to_all | solution.py:85
  261.1 8.7 %all-to-all-start.3 = ((bf16[32,12,1792]{2,1,0:T(8,128)(2,1)}), bf16[32,12,1792]{2,1,0:T(8,128)(2,1)S(1)}, u32[]{:S(2)}, u32[]{:S(2)}) async-start(bf16[32,12,1792]{2,1,0:T(8,128)(2,1)} %reshape.46), calls=%async_computation.3 | async-start | bytes 3670016 | tf_op jit(solution)/shard_map/all_to_all | solution.py:78
  269.9 2.4 select_reduce_fusion
  272.3 4.0 %convert_reduce_fusion = f32[256,1792]{1,0:T(8,128)} fusion(bf16[256,4,1792]{2,0,1:T(8,128)(2,1)} %all-to-all-done), kind=kLoop, calls=%fused_computation.2 | loop fusion | flops 3211264 | bytes 5505024 | tf_op jit(solution)/shard_map/reduce_sum | solution.py:88
  276.3 19.0 %all-to-all-done.3 = bf16[32,12,1792]{2,1,0:T(8,128)(2,1)S(1)} async-done(((bf16[32,12,1792]{2,1,0:T(8,128)(2,1)}), bf16[32,12,1792]{2,1,0:T(8,128)(2,1)S(1)}, u32[]{:S(2)}, u32[]{:S(2)}) %all-to-all-start.3) | async-done | bytes 1376288 | tf_op jit(solution)/shard_map/all_to_all | solution.py:78
  295.6 2.3 convolution_add_fusion.1
  297.9 1.6 fusion.7
  (30 shorter events, 7.0 us)
Async XLA Ops:
  6.5 102.2 %all-gather.5.cloned.1.call-start = ((), (), s32[]{:S(2)}) async-start(), calls=%async_computation.5 | async-start | bytes 6881280 | tf_op jit(solution)/shard_map/all_gather | solution.py:64
  51.8 126.6 %all-gather.3.cloned.1.call-start = ((), (), s32[]{:S(2)}) async-start(), calls=%async_computation.4 | async-start | bytes 4587520 | tf_op jit(solution)/shard_map/all_gather | solution.py:35
  108.7 5.4 %copy-start.3 = (bf16[384,7168]{1,0:T(8,128)(2,1)S(1)}, bf16[384,7168]{1,0:T(8,128)(2,1)}, u32[]{:S(2)}) copy-start(bf16[384,7168]{1,0:T(8,128)(2,1)} %all-gather.5.cloned.1.call-done) | copy-start | bytes 16515076
  108.7 6.3 %copy-start.4 = (bf16[1,7168,256]{2,1,0:T(8,128)(2,1)S(1)}, bf16[1,7168,256]{2,1,0:T(8,128)(2,1)}, u32[]{:S(2)}) copy-start(bf16[1,7168,256]{2,1,0:T(8,128)(2,1)} %param.20) | copy-start | bytes 11010052
  115.1 2.0 copy-start
  121.5 92.2 %all-to-all-start.2 = ((bf16[384,4,1792]{2,0,1:T(8,128)(2,1)}), bf16[384,4,1792]{2,0,1:T(8,128)(2,1)}, u32[]{:S(2)}, u32[]{:S(2)}) async-start(bf16[384,4,1792]{2,0,1:T(8,128)(2,1)} %bitcast.52), calls=%async_computation.2 | async-start | bytes 11010048 | tf_op jit(solution)/shard_map/all_to_all | solution.py:74
  213.8 47.3 %all-to-all-start = ((bf16[256,4,1792]{2,0,1:T(8,128)(2,1)}), bf16[256,4,1792]{2,0,1:T(8,128)(2,1)}, u32[]{:S(2)}, u32[]{:S(2)}) async-start(bf16[256,4,1792]{2,0,1:T(8,128)(2,1)} %bitcast.55), calls=%async_computation | async-start | bytes 7340032 | tf_op jit(solution)/shard_map/all_to_all | solution.py:85
  222.7 47.0 %copy-start.2 = (f32[256,8]{0,1:T(8,128)S(1)}, f32[256,8]{0,1:T(8,128)}, u32[]{:S(2)}) copy-start(f32[256,8]{0,1:T(8,128)} %param.14) | copy-start | bytes 24580
  261.1 34.2 %all-to-all-start.3 = ((bf16[32,12,1792]{2,1,0:T(8,128)(2,1)}), bf16[32,12,1792]{2,1,0:T(8,128)(2,1)S(1)}, u32[]{:S(2)}, u32[]{:S(2)}) async-start(bf16[32,12,1792]{2,1,0:T(8,128)(2,1)} %reshape.46), calls=%async_computation.3 | async-start | bytes 3670016 | tf_op jit(solution)/shard_map/all_to_all | solution.py:78
  295.6 2.3 copy-start.1
Sparse Core Ops, SparseCore 0:
  52.0 56.7 all-gather.4
  110.4 67.9 all-gather.2

commit v2 on v0

v2 whole, which is shorter than its diff:
```python
import functools

import jax
import jax.numpy as jnp
from jax import lax
from jax.experimental import pallas as pl
from jax.experimental.pallas import tpu as pltpu
from jax.sharding import PartitionSpec as P

MOST_R = 12
MESH = pl.DeviceIdType.MESH
BF16 = jnp.bfloat16
F32 = jnp.float32
TP = 4
CHUNKS = 4


def dot(a, b):
    return jnp.dot(a, b, preferred_element_type=F32)


def silu(v):
    return v / (1.0 + jnp.exp(-v))


def slot_parts(shape, axis):
    at = lax.broadcasted_iota(jnp.int32, shape, axis)
    group = (at * 2731) >> 16
    place = at - group * (2 * MOST_R)
    half = (place >= MOST_R).astype(jnp.int32)
    return group, half, place - MOST_R * half


def kernel(
    groups,
    routes_ref,
    routes_t_ref,
    weights_ref,
    placement_row_ref,
    placement_col_ref,
    length_ref,
    hidden_ref,
    sg_ref,
    su_ref,
    sd_ref,
    eg_ref,
    eu_ref,
    ed_ref,
    out_ref,
    wsgu,
    wsd,
    wgu,
    wed,
    held,
    sel,
    back_hi,
    back_lo,
    outgoing,
    arrived,
    acc,
    shared_acc,
    hid2,
    s_part,
    s_own,
    s_relay,
    s_left,
    s_right,
    e_relay,
    e_left,
    e_right,
    came,
    w_sem,
    ag_send,
    ag_recv,
    d_send,
    d_recv,
    d_loc,
    s_send,
    s_recv,
    e_send,
    e_recv,
    c_sem,
):
    dp = lax.axis_index("dp")
    tp = lax.axis_index("tp")
    right = lax.rem(tp + 1, TP)
    left = lax.rem(tp + TP - 1, TP)
    across = lax.rem(tp + 2, TP)
    rows = held.shape[1] // 2
    wide = held.shape[2]
    window = placement_row_ref.shape[1]
    hidden_units = ed_ref.shape[0]
    per_chunk = groups // CHUNKS
    chunk_rows = per_chunk * 2 * MOST_R
    packed = groups * 2 * MOST_R
    top = routes_ref.shape[1]
    owners = (tp, left, right, across)

    for half in range(2):
        pltpu.make_async_copy(
            hidden_ref.at[:, pl.ds(half * wide, wide)],
            held.at[0, pl.ds(half * rows, rows)],
            w_sem.at[0],
        ).start()
    for at, (gate, up, both) in enumerate(((sg_ref, su_ref, wsgu), (eg_ref, eu_ref, wgu))):
        for part, source in enumerate((gate, up)):
            pltpu.make_async_copy(
                source,
                both.at[:, :, pl.ds(part * hidden_units, hidden_units)],
                w_sem.at[1 + at],
            ).start()
    for at, (down, kept) in enumerate(((sd_ref, wsd), (ed_ref, wed))):
        for piece in range(2 * TP):
            pltpu.make_async_copy(
                down.at[:, pl.ds(piece * wide, wide)],
                kept.at[piece // 2, pl.ds((piece % 2) * hidden_units, hidden_units)],
                w_sem.at[3 + at],
            ).start()

    def arrived_weights(ref, at):
        pltpu.make_async_copy(ref, ref, w_sem.at[at]).wait()

    barrier = pltpu.get_barrier_semaphore()

    @pl.loop(1, groups)
    def _(step):
        pl.semaphore_signal(
            barrier,
            inc=1,
            device_id=(lax.rem(dp + step, groups), tp),
            device_id_type=MESH,
        )

    for neighbour in (left, right):
        pl.semaphore_signal(barrier, inc=1, device_id=(dp, neighbour), device_id_type=MESH)

    length = length_ref[0]
    live = lax.broadcasted_iota(jnp.int32, (window, rows), 1) < length
    expert_at = lax.broadcasted_iota(jnp.int32, (window, rows), 0)
    named = jnp.zeros((window, rows), F32)
    for k in range(top):
        named = named + jnp.where(routes_t_ref[pl.ds(k, 1), :] == expert_at, 1.0, 0.0)
    named = jnp.where(live, named, 0.0)
    before = jnp.where(
        lax.broadcasted_iota(jnp.int32, (rows, rows), 0)
        < lax.broadcasted_iota(jnp.int32, (rows, rows), 1),
        1.0,
        0.0,
    ).astype(BF16)
    place = jnp.where(named > 0.0, dot(named.astype(BF16), before), -1.0).astype(BF16)
    group_of, _, _ = slot_parts((packed, window), 0)
    spread = jnp.where(placement_row_ref[...] == group_of, 1.0, 0.0).astype(BF16)
    _, half_of, want = slot_parts((packed, rows), 0)
    hit = dot(spread, place) == want.astype(F32)
    for half in range(2):
        sel[:, pl.ds(half * rows, rows)] = jnp.where(
            hit, jnp.where(half_of == half, 1.0, 0.0), 0.0
        ).astype(BF16)

    pl.semaphore_wait(barrier, groups - 1 + 2)

    def to(src, dst, send, recv, device):
        return pltpu.make_async_remote_copy(
            src_ref=src,
            dst_ref=dst,
            send_sem=send,
            recv_sem=recv,
            device_id=device,
            device_id_type=MESH,
        )

    arrived_weights(held.at[0], 0)

    def half_block(slot, half):
        return held.at[slot, pl.ds(half * rows, rows)]

    gathers = []
    for at, (source, target, half, device) in enumerate(
        (
            (0, 1, 0, right),
            (0, 2, 1, left),
            (0, 1, 1, right),
            (0, 2, 0, left),
            (1, 3, 0, right),
            (2, 3, 1, left),
        )
    ):
        gathers.append(
            to(
                half_block(source, half),
                half_block(target, half),
                ag_send.at[at],
                ag_recv.at[at],
                (dp, device),
            )
        )
    for at in range(4):
        gathers[at].start()

    my_chunk = dp // per_chunk

    def chunk_at(k):
        return lax.rem(my_chunk + k, CHUNKS)

    def send_chunk(source, landing, chunk, send, recv, local):
        @pl.loop(0, per_chunk)
        def _(step):
            target = chunk * per_chunk + lax.rem(dp + step, per_chunk)

            @pl.when(target != dp)
            def _():
                to(source.at[target], landing.at[dp], send, recv, (target, tp)).start()

            @pl.when(target == dp)
            def _():
                pltpu.make_async_copy(source.at[dp], landing.at[dp], local).start()

    def wait_peers(ref, sem):
        view = ref.at[pl.ds(0, groups - 1)]
        pltpu.make_async_copy(view, view, sem).wait()

    def select(slot):
        @pl.loop(0, CHUNKS)
        def _(k):
            chunk = chunk_at(k)
            picked = dot(
                sel[pl.ds(pl.multiple_of(chunk * chunk_rows, chunk_rows), chunk_rows), :],
                held[slot],
            )
            outgoing[slot, pl.ds(chunk * per_chunk, per_chunk)] = picked.reshape(
                per_chunk, 2 * MOST_R, wide
            ).astype(BF16)
            send_chunk(
                outgoing.at[slot],
                arrived.at[slot],
                chunk,
                d_send.at[slot],
                d_recv.at[slot],
                d_loc.at[slot],
            )

    def shared_step(slot):
        owner = owners[slot]
        total = dot(held[slot, pl.ds(0, rows)], wsgu[2 * owner]) + dot(
            held[slot, pl.ds(rows, rows)], wsgu[2 * owner + 1]
        )
        if slot == 0:
            shared_acc[...] = total
        else:
            shared_acc[...] += total

    def load_chunk(ref, k):
        return ref[pl.ds(k * per_chunk, per_chunk)].astype(F32).reshape(chunk_rows, wide)

    def rows_of(chunk):
        return pl.ds(pl.multiple_of(chunk * chunk_rows, chunk_rows), chunk_rows)

    select(0)
    arrived_weights(wsgu, 1)
    shared_step(0)

    expert_at = lax.broadcasted_iota(jnp.int32, (rows, window), 1)
    live = lax.broadcasted_iota(jnp.int32, (rows, window), 0) < length
    named = jnp.zeros((rows, window), F32)
    scale = jnp.zeros((rows, window), F32)
    for k in range(top):
        match = routes_ref[:, pl.ds(k, 1)] == expert_at
        named = named + jnp.where(match, 1.0, 0.0)
        scale = scale + jnp.where(match, weights_ref[:, pl.ds(k, 1)], 0.0)
    named = jnp.where(live, named, 0.0)
    before = jnp.where(
        lax.broadcasted_iota(jnp.int32, (rows, rows), 1)
        < lax.broadcasted_iota(jnp.int32, (rows, rows), 0),
        1.0,
        0.0,
    ).astype(BF16)
    place = jnp.where(named > 0.0, dot(before, named.astype(BF16)), -1.0).astype(BF16)
    group_of, _, _ = slot_parts((window, packed), 1)
    spread = jnp.where(placement_col_ref[...] == group_of, 1.0, 0.0).astype(BF16)
    _, half_of, want = slot_parts((rows, packed), 1)
    hit = dot(place, spread) == want.astype(F32)
    head = scale.astype(BF16)
    rest = (scale - head.astype(F32)).astype(BF16)
    for part, kept in ((head, back_hi), (rest, back_lo)):
        value = jnp.where(hit, dot(part, spread), 0.0)
        for half in range(2):
            kept[pl.ds(half * rows, rows), :] = jnp.where(half_of == half, value, 0.0).astype(BF16)

    for at in (0, 1):
        gathers[at].wait_recv()
        gathers[at + 4].start()
    for slot in (1, 2):
        gathers[slot + 1].wait_recv()
        select(slot)
        shared_step(slot)
    for at in (4, 5):
        gathers[at].wait_recv()
    select(3)
    shared_step(3)

    shared_hidden = (
        silu(shared_acc[:, pl.ds(0, hidden_units)])
        * shared_acc[:, pl.ds(hidden_units, hidden_units)]
    ).astype(BF16)
    arrived_weights(wsd, 3)
    for at, owner in ((0, across), (1, right), (2, left), (3, tp)):
        for half in range(2):
            part = dot(shared_hidden, wsd[owner, pl.ds(half * hidden_units, hidden_units)])
            if at < 3:
                s_part[at, pl.ds(half * rows, rows)] = part.astype(BF16)
            else:
                s_own[pl.ds(half * rows, rows)] = part

    def s_copy(at, part, half, landing, device):
        where = pl.ds(half * rows, rows)
        return to(
            s_part.at[part, where],
            landing.at[where],
            s_send.at[at],
            s_recv.at[at],
            (dp, device),
        )

    shared_sends = [
        s_copy(0, 0, 0, s_relay, right),
        s_copy(1, 0, 1, s_relay, left),
        s_copy(2, 1, 1, s_left, right),
        s_copy(3, 2, 0, s_right, left),
        s_copy(4, 1, 0, s_left, right),
        s_copy(5, 2, 1, s_right, left),
    ]
    for at in range(4):
        shared_sends[at].start()

    both = 2 * hidden_units

    def expert_step(slot):
        wait_peers(arrived.at[slot], d_recv.at[slot])
        pltpu.make_async_copy(arrived.at[slot, 0], arrived.at[slot, 0], d_loc.at[slot]).wait()
        owner = owners[slot]

        @pl.loop(0, CHUNKS)
        def _(k):
            block = load_chunk(arrived.at[slot], k).astype(BF16)
            for half in range(2):
                where = (rows_of(k), pl.ds(half * both, both))
                total = dot(block, wgu[2 * owner + half])
                if slot == 0:
                    acc[where] = total
                else:
                    acc[where] += total

    arrived_weights(wgu, 2)
    expert_step(0)
    for at, part, half in ((0, 1, 0), (1, 2, 1)):
        shared_sends[at].wait_recv()
        where = pl.ds(half * rows, rows)
        s_part[part, where] = (
            s_part[part, where].astype(F32) + s_relay[where].astype(F32)
        ).astype(BF16)
        shared_sends[at + 4].start()
    expert_step(1)
    expert_step(2)
    arrived_weights(wed, 4)
    for at in range(2, 6):
        shared_sends[at].wait_recv()
    s_own[...] = s_own[...] + s_left[...].astype(F32) + s_right[...].astype(F32)
    for slot in range(4):
        wait_peers(outgoing.at[slot], d_send.at[slot])
    expert_step(3)

    @pl.loop(0, CHUNKS)
    def _(k):
        first = acc[rows_of(k), pl.ds(0, both)]
        second = acc[rows_of(k), pl.ds(both, both)]
        total = first + pltpu.roll(second, chunk_rows - MOST_R, 0)
        inner = silu(total[:, :hidden_units]) * total[:, hidden_units:]
        _, half_of, _ = slot_parts((chunk_rows, hidden_units), 0)
        hid2[rows_of(k), pl.ds(0, hidden_units)] = jnp.where(half_of == 0, inner, 0.0).astype(BF16)
        hid2[rows_of(k), pl.ds(hidden_units, hidden_units)] = jnp.where(
            half_of == 1, pltpu.roll(inner, MOST_R, 0), 0.0
        ).astype(BF16)

    def down(slot, owner, k):
        chunk = chunk_at(k)
        part = dot(hid2[rows_of(chunk), :], wed[owner])
        if slot:
            outgoing[slot, pl.ds(chunk * per_chunk, per_chunk)] = part.reshape(
                per_chunk, 2 * MOST_R, wide
            ).astype(BF16)
        else:
            acc[rows_of(chunk), pl.ds(0, wide)] = part

    def e_copy(at, slot, k, landing, device):
        where = pl.ds(chunk_at(k) * per_chunk, per_chunk)
        return to(
            outgoing.at[slot, where],
            landing.at[where],
            e_send.at[at],
            e_recv.at[at],
            (dp, device),
        )

    relays = [e_copy(k, 1, k, e_relay, right if k < 2 else left) for k in range(4)]
    directs = [
        e_copy(4 + k, 3 if k < 2 else 2, k, e_right if k < 2 else e_left, left if k < 2 else right)
        for k in range(4)
    ]
    passed = [
        e_copy(8 + k, 2 if k < 2 else 3, k, e_left if k < 2 else e_right, right if k < 2 else left)
        for k in range(4)
    ]
    for k in (0, 2, 1, 3):
        down(1, across, k)
        relays[k].start()
    for k in (2, 0, 3, 1):
        down(2 if k >= 2 else 3, right if k >= 2 else left, k)
        directs[k].start()
    for k in (0, 2, 1, 3):
        down(2 if k < 2 else 3, right if k < 2 else left, k)
    for k in (0, 2, 1, 3):
        slot = 2 if k < 2 else 3
        where = pl.ds(chunk_at(k) * per_chunk, per_chunk)
        relays[k].wait_recv()
        outgoing[slot, where] = (
            outgoing[slot, where].astype(F32) + e_relay[where].astype(F32)
        ).astype(BF16)
        passed[k].start()
    for k in (0, 2, 1, 3):
        down(0, tp, k)
    for k in (0, 2, 1, 3):
        chunk = chunk_at(k)
        directs[k].wait_recv()
        passed[k].wait_recv()
        total = (
            acc[rows_of(chunk), pl.ds(0, wide)]
            + load_chunk(e_left, chunk)
            + load_chunk(e_right, chunk)
        )
        outgoing[0, pl.ds(chunk * per_chunk, per_chunk)] = total.reshape(
            per_chunk, 2 * MOST_R, wide
        ).astype(BF16)
        send_chunk(outgoing.at[0], came, chunk, c_sem.at[0], c_sem.at[1], c_sem.at[2])

    wait_peers(came, c_sem.at[1])
    pltpu.make_async_copy(came.at[0], came.at[0], c_sem.at[2]).wait()
    for k in range(CHUNKS):
        block = load_chunk(came, k).astype(BF16)
        where = pl.ds(k * chunk_rows, chunk_rows)
        s_own[...] += dot(back_hi[:, where], block) + dot(back_lo[:, where], block)
    keep = lax.broadcasted_iota(jnp.int32, (rows, wide), 0) < length
    for half in range(2):
        out_ref[:, pl.ds(half * wide, wide)] = jnp.where(
            keep, s_own[pl.ds(half * rows, rows)], 0.0
        ).astype(out_ref.dtype)

    for copy in gathers + shared_sends + relays + directs + passed:
        copy.wait_send()
    wait_peers(outgoing.at[0], c_sem.at[0])


def local(
    hidden_in,
    lengths,
    routes,
    route_weights,
    placement,
    shared_gate,
    shared_up,
    shared_down,
    expert_gate,
    expert_up,
    expert_down,
):
    groups = lax.axis_size("dp")
    rows, quarter = hidden_in.shape
    wide = quarter // 2
    pieces = 2 * TP
    units = shared_gate.shape[1]
    window = placement.shape[0]
    packed = groups * 2 * MOST_R
    across_peers = (groups, 2 * MOST_R, wide)
    vmem = pl.BlockSpec(memory_space=pltpu.VMEM)
    smem = pl.BlockSpec(memory_space=pltpu.SMEM)
    hbm = pl.BlockSpec(memory_space=pl.ANY)
    dma = pltpu.SemaphoreType.DMA
    return pl.pallas_call(
        functools.partial(kernel, groups),
        out_shape=jax.ShapeDtypeStruct((rows, quarter), BF16),
        in_specs=[vmem] * 5 + [smem] + [hbm] * 7,
        out_specs=vmem,
        scratch_shapes=[
            pltpu.VMEM((pieces, wide, 2 * units), BF16),
            pltpu.VMEM((TP, 2 * units, wide), BF16),
            pltpu.VMEM((pieces, wide, 2 * units), BF16),
            pltpu.VMEM((TP, 2 * units, wide), BF16),
            pltpu.VMEM((TP, 2 * rows, wide), BF16),
            pltpu.VMEM((packed, 2 * rows), BF16),
            pltpu.VMEM((2 * rows, packed), BF16),
            pltpu.VMEM((2 * rows, packed), BF16),
            pltpu.VMEM((TP,) + across_peers, BF16),
            pltpu.VMEM((TP,) + across_peers, BF16),
            pltpu.VMEM((packed, 4 * units), F32),
            pltpu.VMEM((rows, 2 * units), F32),
            pltpu.VMEM((packed, 2 * units), BF16),
            pltpu.VMEM((3, 2 * rows, wide), BF16),
            pltpu.VMEM((2 * rows, wide), F32),
            pltpu.VMEM((2 * rows, wide), BF16),
            pltpu.VMEM((2 * rows, wide), BF16),
            pltpu.VMEM((2 * rows, wide), BF16),
            pltpu.VMEM(across_peers, BF16),
            pltpu.VMEM(across_peers, BF16),
            pltpu.VMEM(across_peers, BF16),
            pltpu.VMEM(across_peers, BF16),
            dma((5,)),
            dma((6,)),
            dma((6,)),
            dma((TP,)),
            dma((TP,)),
            dma((TP,)),
            dma((6,)),
            dma((6,)),
            dma((12,)),
            dma((12,)),
            dma((3,)),
        ],
        compiler_params=pltpu.CompilerParams(
            collective_id=0, has_side_effects=True, vmem_limit_bytes=62 << 20
        ),
        cost_estimate=pl.CostEstimate(
            flops=2 * 5 * rows * quarter * 4 * units * 3 // 2,
            bytes_accessed=6 * quarter * 4 * units * 2,
            transcendentals=0,
        ),
    )(
        routes,
        routes.T,
        route_weights,
        placement.reshape(1, window),
        placement.reshape(window, 1),
        lengths,
        hidden_in,
        shared_gate.reshape(pieces, wide, units),
        shared_up.reshape(pieces, wide, units),
        shared_down,
        expert_gate.reshape(pieces, wide, units),
        expert_up.reshape(pieces, wide, units),
        expert_down[0],
    )


def solution(mesh):
    in_specs = (
        P("dp", "tp"),
        P("dp"),
        P("dp", None),
        P("dp", None),
        P(),
        P(None, "tp"),
        P(None, "tp"),
        P("tp", None),
        P("dp", None, "tp"),
        P("dp", None, "tp"),
        P("dp", "tp", None),
    )
    out_specs = P("dp", "tp")
    return jax.shard_map(local, mesh=mesh, in_specs=in_specs, out_specs=out_specs, check_vma=False)
```

time: 611 us -> 153 us (0.25)
  waiting for transfers between devices: 357 us -> 0 us
  Pallas kernels: 0 us -> 145 us
  local copies, waits for them, and re-layouts: 138 us -> 6.47 us
  matrix products: 48.8 us -> 0 us
  blocking collectives: 35.1 us -> 0 us
  between operations: 14.2 us -> 0.66 us
  starting transfers between devices: 7.8 us -> 0 us
  other arithmetic: 7.27 us -> 0 us
    all_to_all x1 -> x0, waiting for transfers between devices: 150 us -> none  [local(): lax.all_to_all(expert_part.reshape(groups, per_peer, full_width), 'dp', s...]
    pallas_call x0 -> x1, Pallas kernels: none -> 145 us  [local(): pl.pallas_call(functools.partial(kernel, groups), out_shape=jax.ShapeDtyp...]
    gather x8 -> x0, local copies, waits for them, and re-layouts: 104 us -> none  [weighted_pick(): returned_rows[safe_index[:, route]]]
    reduce_scatter x1 -> x0, waiting for transfers between devices: 104 us -> none  [local(): combined = lax.psum_scatter(summands, 'tp', scatter_dimension=1, tiled=True)]
    all_gather x2 -> x0, waiting for transfers between devices: 102 us -> none  [the longest x1 56.9 us: local(): lax.all_gather(arrived.reshape(slot_count, quarter), 'tp', axis=1, tiled=...]
    dot_general x6 -> x0, matrix products: 48.8 us -> none  [the longest x1 27.3 us: local(): jnp.dot(gated_hidden(shared_gate_sum, shared_up_sum), shared_down, prefer...]
    all_to_all x1 -> x0, blocking collectives: 35.1 us -> none  [local(): lax.all_to_all(outgoing.reshape(groups, per_peer, quarter), 'dp', split_a...]
    dot_general x2 -> x0, local copies, waits for them, and re-layouts: 15.9 us -> none  [local(): jnp.dot(gated_hidden(expert_gate_sum, expert_up_sum), expert_down[0], pre...]
  transfers between devices with their start and end apart: 4 -> 0, of which waited for: 4 -> 0; matrix products, arithmetic and copies ran while one was open for 1% -> 0% of each run, Pallas kernels for 0% -> 0%
where the time goes in v2:
time: 153 us
  Pallas kernels  145 us (95%)
  local copies, waits for them, and re-layouts  6.47 us (4%)
    pallas_call x1, Pallas kernels, local(): pl.pallas_call(functools.partial(kernel, groups), out_shape=jax.ShapeDtyp...  145 us
    unnamed x3, local copies, waits for them, and re-layouts  5.14 us

profile of v2, /device:TPU:1, one launch (start us, length us, event | category | flops | bytes accessed | tf_op | source)
XLA Modules:
  0.0 152.6 jit_solution(5975985880448340041)
XLA Ops:
  0.7 1.3 copy.14.placement_col_ref
  2.0 1.5 copy.13.weights_ref
  3.5 1.5 copy.12.routes_ref
  5.0 145.4 %shard_map.109 = bf16[256,1792]{1,0:T(8,128)(2,1)} custom-call(s32[256,8]{1,0:T(8,128)} %copy.12.routes_ref, s32[8,256]{1,0:T(8,128)} %bitcast.8, f32[256,8]{1,0:T(8,128)} %copy.13.weights_ref, s32[1,32]{1,0:T(1,128)} %bitcast.10, s32[32,1]{1,0:T(8,128)} %copy.14.placement_col_ref, s32[1]{0:T(128)S(6)} %copy.16.length_ref, bf16[256,1792]{1,0:T(8,128)(2,1)} %hidden_ref.1, ...), custom_call_target="tpu_custom_call" | custom-call | flops 7046430720 | bytes 22020096 | tf_op jit(solution)/shard_map/pallas_call | solution.py:487
  150.4 2.2 %copy.17 = bf16[256,1792]{1,0:T(8,128)(2,1)} copy(bf16[256,1792]{1,0:T(8,128)(2,1)} %shard_map.109) | data formatting | bytes 1835008

commit v3 on v2

v3 whole, which is shorter than its diff:
```python
import functools

import jax
import jax.numpy as jnp
from jax import lax
from jax.experimental import pallas as pl
from jax.experimental.pallas import tpu as pltpu
from jax.sharding import PartitionSpec as P

MOST_R = 12
MESH = pl.DeviceIdType.MESH
BF16 = jnp.bfloat16
F32 = jnp.float32
TP = 4
CHUNKS = 4


def dot(a, b):
    return jnp.dot(a, b, preferred_element_type=F32)


def silu(v):
    return v / (1.0 + jnp.exp(-v))


def slot_parts(shape, axis):
    at = lax.broadcasted_iota(jnp.int32, shape, axis)
    group = (at * 2731) >> 16
    place = at - group * (2 * MOST_R)
    half = (place >= MOST_R).astype(jnp.int32)
    return group, half, place - MOST_R * half


def kernel(
    groups,
    routes_ref,
    weights_ref,
    placement_ref,
    length_ref,
    hidden_ref,
    sg_ref,
    su_ref,
    sd_ref,
    eg_ref,
    eu_ref,
    ed_ref,
    out_ref,
    wsgu,
    wsd,
    wgu,
    wed,
    held,
    sel,
    back_hi,
    back_lo,
    outgoing,
    arrived,
    acc,
    shared_acc,
    hid2,
    s_part,
    s_own,
    s_relay,
    s_left,
    s_right,
    e_relay,
    e_left,
    e_right,
    came,
    w_sem,
    ag_send,
    ag_recv,
    d_send,
    d_recv,
    d_loc,
    s_send,
    s_recv,
    e_send,
    e_recv,
    c_send,
    c_recv,
    c_loc,
):
    dp = lax.axis_index("dp")
    tp = lax.axis_index("tp")
    right = lax.rem(tp + 1, TP)
    left = lax.rem(tp + TP - 1, TP)
    across = lax.rem(tp + 2, TP)
    rows = held.shape[1] // 2
    wide = held.shape[2]
    window = placement_ref.shape[1]
    hidden_units = ed_ref.shape[0]
    per_chunk = groups // CHUNKS
    chunk_rows = per_chunk * 2 * MOST_R
    packed = groups * 2 * MOST_R
    top = routes_ref.shape[0]
    pieces = (
        (2 * tp, 2 * tp + 1),
        (2 * left, 2 * right + 1),
        (2 * left + 1, 2 * right),
        (2 * across, 2 * across + 1),
    )

    for half in range(2):
        pltpu.make_async_copy(
            hidden_ref.at[:, pl.ds(half * wide, wide)],
            held.at[0, pl.ds(half * rows, rows)],
            w_sem.at[0],
        ).start()
    for at, (gate, up, both) in enumerate(((sg_ref, su_ref, wsgu), (eg_ref, eu_ref, wgu))):
        for part, source in enumerate((gate, up)):
            pltpu.make_async_copy(
                source,
                both.at[:, :, pl.ds(part * hidden_units, hidden_units)],
                w_sem.at[1 + at],
            ).start()
    for at, (down, kept) in enumerate(((sd_ref, wsd), (ed_ref, wed))):
        for piece in range(2 * TP):
            pltpu.make_async_copy(
                down.at[:, pl.ds(piece * wide, wide)],
                kept.at[piece // 2, pl.ds((piece % 2) * hidden_units, hidden_units)],
                w_sem.at[3 + at],
            ).start()

    def arrived_weights(ref, at):
        pltpu.make_async_copy(ref, ref, w_sem.at[at]).wait()

    barrier = pltpu.get_barrier_semaphore()

    @pl.loop(1, groups)
    def _(step):
        pl.semaphore_signal(
            barrier,
            inc=1,
            device_id=(lax.rem(dp + step, groups), tp),
            device_id_type=MESH,
        )

    for neighbour in (left, right):
        pl.semaphore_signal(barrier, inc=1, device_id=(dp, neighbour), device_id_type=MESH)

    length = length_ref[0]
    live = lax.broadcasted_iota(jnp.int32, (window, rows), 1) < length
    expert_at = lax.broadcasted_iota(jnp.int32, (window, rows), 0)
    named = jnp.zeros((window, rows), F32)
    scale = jnp.zeros((window, rows), F32)
    for k in range(top):
        match = routes_ref[pl.ds(k, 1), :] == expert_at
        named = named + jnp.where(match, 1.0, 0.0)
        scale = scale + jnp.where(match, weights_ref[pl.ds(k, 1), :], 0.0)
    named = jnp.where(live, named, 0.0)
    before = jnp.where(
        lax.broadcasted_iota(jnp.int32, (rows, rows), 0)
        < lax.broadcasted_iota(jnp.int32, (rows, rows), 1),
        1.0,
        0.0,
    ).astype(BF16)
    place = jnp.where(named > 0.0, dot(named.astype(BF16), before), -1.0)
    group_of, _, _ = slot_parts((packed, window), 0)
    spread = jnp.where(placement_ref[...] == group_of, 1.0, 0.0).astype(BF16)
    _, half_of, want = slot_parts((packed, rows), 0)
    hit = dot(spread, place.astype(BF16)) == want.astype(F32)
    for half in range(2):
        sel[:, pl.ds(half * rows, rows)] = jnp.where(
            hit, jnp.where(half_of == half, 1.0, 0.0), 0.0
        ).astype(BF16)

    pl.semaphore_wait(barrier, groups - 1 + 2)

    def to(src, dst, send, recv, device):
        return pltpu.make_async_remote_copy(
            src_ref=src,
            dst_ref=dst,
            send_sem=send,
            recv_sem=recv,
            device_id=device,
            device_id_type=MESH,
        )

    arrived_weights(held.at[0], 0)

    def half_block(slot, half):
        return held.at[slot, pl.ds(half * rows, rows)]

    gathers = []
    for at, (source, half, target, landing, device) in enumerate(
        (
            (0, 0, 1, 0, right),
            (0, 1, 1, 1, left),
            (0, 1, 2, 0, right),
            (0, 0, 2, 1, left),
            (1, 0, 3, 0, right),
            (1, 1, 3, 1, left),
        )
    ):
        gathers.append(
            to(
                half_block(source, half),
                half_block(target, landing),
                ag_send.at[at],
                ag_recv.at[at],
                (dp, device),
            )
        )
    for at in range(2):
        gathers[at].start()

    my_chunk = dp // per_chunk

    def chunk_at(k):
        return lax.rem(my_chunk + k, CHUNKS)

    def send_chunk(source, landing, chunk, send, recv, local):
        @pl.loop(0, per_chunk)
        def _(step):
            target = chunk * per_chunk + lax.rem(dp + step, per_chunk)

            @pl.when(target != dp)
            def _():
                to(source.at[target], landing.at[dp], send, recv, (target, tp)).start()

            @pl.when(target == dp)
            def _():
                pltpu.make_async_copy(source.at[dp], landing.at[dp], local).start()

    def wait_peers(ref, sem, number):
        view = ref.at[pl.ds(0, number)]
        pltpu.make_async_copy(view, view, sem).wait()

    def from_chunk(k):
        return lax.rem(my_chunk + CHUNKS - k, CHUNKS)

    def wait_chunk(ref, k, recv, local):
        wait_peers(ref, recv.at[k], per_chunk - 1 if k == 0 else per_chunk)
        if k == 0:
            wait_peers(ref, local, 1)

    def select(slot):
        @pl.loop(0, CHUNKS)
        def _(k):
            chunk = chunk_at(k)
            picked = dot(
                sel[pl.ds(pl.multiple_of(chunk * chunk_rows, chunk_rows), chunk_rows), :],
                held[slot],
            )
            outgoing[slot, pl.ds(chunk * per_chunk, per_chunk)] = picked.reshape(
                per_chunk, 2 * MOST_R, wide
            ).astype(BF16)
            send_chunk(
                outgoing.at[slot],
                arrived.at[slot],
                chunk,
                d_send.at[slot],
                d_recv.at[slot, k],
                d_loc.at[slot],
            )

    def shared_step(slot):
        first, second = pieces[slot]
        total = dot(held[slot, pl.ds(0, rows)], wsgu[first]) + dot(
            held[slot, pl.ds(rows, rows)], wsgu[second]
        )
        if slot == 0:
            shared_acc[...] = total
        else:
            shared_acc[...] += total

    def load_chunk(ref, k):
        return ref[pl.ds(k * per_chunk, per_chunk)].astype(F32).reshape(chunk_rows, wide)

    def rows_of(chunk):
        return pl.ds(pl.multiple_of(chunk * chunk_rows, chunk_rows), chunk_rows)

    select(0)
    arrived_weights(wsgu, 1)
    shared_step(0)

    place = jnp.transpose(place).astype(BF16)
    scale = jnp.transpose(scale)
    head = scale.astype(BF16)
    rest = (scale - head.astype(F32)).astype(BF16)
    placement_col = jnp.transpose(
        jnp.broadcast_to(placement_ref[...].astype(F32), (8, window))
    )[:, :1]
    for chunk in range(CHUNKS):
        group_of, _, _ = slot_parts((window, chunk_rows), 1)
        group_of = (group_of + chunk * per_chunk).astype(F32)
        spread = jnp.where(placement_col == group_of, 1.0, 0.0).astype(BF16)
        _, half_of, want = slot_parts((rows, chunk_rows), 1)
        hit = dot(place, spread) == want.astype(F32)
        for part, kept in ((head, back_hi), (rest, back_lo)):
            value = jnp.where(hit, dot(part, spread), 0.0)
            for half in range(2):
                kept[chunk, pl.ds(half * rows, rows), :] = jnp.where(
                    half_of == half, value, 0.0
                ).astype(BF16)

    for at in (0, 1):
        gathers[at].wait_recv()
        gathers[at + 2].start()
        gathers[at + 4].start()
    select(1)
    shared_step(1)
    for slot in (2, 3):
        for at in (0, 1):
            gathers[2 * slot - 2 + at].wait_recv()
        select(slot)
        shared_step(slot)

    shared_hidden = (
        silu(shared_acc[:, pl.ds(0, hidden_units)])
        * shared_acc[:, pl.ds(hidden_units, hidden_units)]
    ).astype(BF16)
    arrived_weights(wsd, 3)
    for at, owner in ((0, across), (1, right), (2, left), (3, tp)):
        for half in range(2):
            part = dot(shared_hidden, wsd[owner, pl.ds(half * hidden_units, hidden_units)])
            if at < 3:
                s_part[at, pl.ds(half * rows, rows)] = part.astype(BF16)
            else:
                s_own[pl.ds(half * rows, rows)] = part

    def s_copy(at, part, half, landing, device):
        where = pl.ds(half * rows, rows)
        return to(
            s_part.at[part, where],
            landing.at[where],
            s_send.at[at],
            s_recv.at[at],
            (dp, device),
        )

    shared_sends = [
        s_copy(0, 0, 0, s_relay, right),
        s_copy(1, 0, 1, s_relay, left),
        s_copy(2, 1, 1, s_left, right),
        s_copy(3, 2, 0, s_right, left),
        s_copy(4, 1, 0, s_left, right),
        s_copy(5, 2, 1, s_right, left),
    ]
    for at in range(2):
        shared_sends[at].start()

    both = 2 * hidden_units

    def expert_chunk(slot, k):
        wait_chunk(arrived.at[slot], k, d_recv.at[slot], d_loc.at[slot])
        chunk = from_chunk(k)
        block = load_chunk(arrived.at[slot], chunk).astype(BF16)
        for half in range(2):
            where = (rows_of(chunk), pl.ds(half * both, both))
            total = dot(block, wgu[pieces[slot][half]])
            if slot == 0:
                acc[where] = total
            else:
                acc[where] += total

    def activate(chunk):
        first = acc[rows_of(chunk), pl.ds(0, both)]
        second = acc[rows_of(chunk), pl.ds(both, both)]
        total = first + pltpu.roll(second, chunk_rows - MOST_R, 0)
        inner = silu(total[:, :hidden_units]) * total[:, hidden_units:]
        _, half_of, _ = slot_parts((chunk_rows, hidden_units), 0)
        hid2[rows_of(chunk), pl.ds(0, hidden_units)] = jnp.where(
            half_of == 0, inner, 0.0
        ).astype(BF16)
        hid2[rows_of(chunk), pl.ds(hidden_units, hidden_units)] = jnp.where(
            half_of == 1, pltpu.roll(inner, MOST_R, 0), 0.0
        ).astype(BF16)

    def down(slot, owner, k):
        chunk = from_chunk(k)
        part = dot(hid2[rows_of(chunk), :], wed[owner])
        if slot is not None:
            outgoing[slot, pl.ds(chunk * per_chunk, per_chunk)] = part.reshape(
                per_chunk, 2 * MOST_R, wide
            ).astype(BF16)
        else:
            acc[rows_of(chunk), pl.ds(0, wide)] = part

    def e_copy(at, slot, k, landing, device):
        where = pl.ds(from_chunk(k) * per_chunk, per_chunk)
        return to(
            outgoing.at[slot, where],
            landing.at[where],
            e_send.at[at],
            e_recv.at[at],
            (dp, device),
        )

    relays, directs, passed = [], [], []
    for k in range(CHUNKS):
        ahead, behind = ((1, right, e_left), (2, left, e_right))[:: 1 if k % 2 == 0 else -1]
        relays.append(e_copy(k, 0, k, e_relay, ahead[1]))
        directs.append(e_copy(4 + k, behind[0], k, behind[2], behind[1]))
        passed.append((ahead, e_copy(8 + k, ahead[0], k, ahead[2], ahead[1])))

    def pass_on(k):
        (slot, _, _), copy = passed[k]
        where = pl.ds(from_chunk(k) * per_chunk, per_chunk)
        relays[k].wait_recv()
        outgoing[slot, where] = (
            outgoing[slot, where].astype(F32) + e_relay[where].astype(F32)
        ).astype(BF16)
        copy.start()

    def finish(k):
        chunk = from_chunk(k)
        down(None, tp, k)
        directs[k].wait_recv()
        passed[k][1].wait_recv()
        total = (
            acc[rows_of(chunk), pl.ds(0, wide)]
            + load_chunk(e_left, chunk)
            + load_chunk(e_right, chunk)
        )
        outgoing[3, pl.ds(chunk * per_chunk, per_chunk)] = total.reshape(
            per_chunk, 2 * MOST_R, wide
        ).astype(BF16)
        send_chunk(outgoing.at[3], came, chunk, c_send.at[0], c_recv.at[k], c_loc.at[0])

    arrived_weights(wgu, 2)
    for k in range(CHUNKS):
        expert_chunk(0, k)
    for at in (2, 3):
        shared_sends[at].start()
    for k in range(CHUNKS):
        expert_chunk(1, k)
    for at, part, half in ((0, 1, 0), (1, 2, 1)):
        shared_sends[at].wait_recv()
        where = pl.ds(half * rows, rows)
        s_part[part, where] = (
            s_part[part, where].astype(F32) + s_relay[where].astype(F32)
        ).astype(BF16)
        shared_sends[at + 4].start()
    for k in range(CHUNKS):
        expert_chunk(2, k)
    arrived_weights(wed, 4)
    for slot in range(3):
        wait_peers(outgoing.at[slot], d_send.at[slot], groups - 1)
    for k in range(CHUNKS):
        expert_chunk(3, k)
        activate(from_chunk(k))
        down(0, across, k)
        relays[k].start()
        slot, device = ((2, left), (1, right))[k % 2]
        down(slot, device, k)
        directs[k].start()
        (slot, device, _), _ = passed[k]
        down(slot, device, k)
        if k:
            pass_on(k - 1)
    pass_on(CHUNKS - 1)
    for at in range(2, 6):
        shared_sends[at].wait_recv()
    s_own[...] = s_own[...] + s_left[...].astype(F32) + s_right[...].astype(F32)
    wait_peers(outgoing.at[3], d_send.at[3], groups - 1)
    for k in range(CHUNKS):
        finish(k)

    for k in range(CHUNKS):
        wait_chunk(came, k, c_recv, c_loc.at[0])
        chunk = chunk_at(k)
        block = load_chunk(came, chunk).astype(BF16)
        s_own[...] += dot(back_hi[chunk], block) + dot(back_lo[chunk], block)
    keep = lax.broadcasted_iota(jnp.int32, (rows, wide), 0) < length
    for half in range(2):
        out_ref[:, pl.ds(half * wide, wide)] = jnp.where(
            keep, s_own[pl.ds(half * rows, rows)], 0.0
        ).astype(out_ref.dtype)

    for copy in gathers + shared_sends + relays + directs + [copy for _, copy in passed]:
        copy.wait_send()
    wait_peers(outgoing.at[3], c_send.at[0], groups - 1)


def local(
    hidden_in,
    lengths,
    routes,
    route_weights,
    placement,
    shared_gate,
    shared_up,
    shared_down,
    expert_gate,
    expert_up,
    expert_down,
):
    groups = lax.axis_size("dp")
    rows, quarter = hidden_in.shape
    wide = quarter // 2
    pieces = 2 * TP
    units = shared_gate.shape[1]
    window = placement.shape[0]
    packed = groups * 2 * MOST_R
    across_peers = (groups, 2 * MOST_R, wide)
    vmem = pl.BlockSpec(memory_space=pltpu.VMEM)
    smem = pl.BlockSpec(memory_space=pltpu.SMEM)
    hbm = pl.BlockSpec(memory_space=pl.ANY)
    dma = pltpu.SemaphoreType.DMA
    return pl.pallas_call(
        functools.partial(kernel, groups),
        out_shape=jax.ShapeDtypeStruct((rows, quarter), BF16),
        in_specs=[vmem] * 3 + [smem] + [hbm] * 7,
        out_specs=vmem,
        scratch_shapes=[
            pltpu.VMEM((pieces, wide, 2 * units), BF16),
            pltpu.VMEM((TP, 2 * units, wide), BF16),
            pltpu.VMEM((pieces, wide, 2 * units), BF16),
            pltpu.VMEM((TP, 2 * units, wide), BF16),
            pltpu.VMEM((TP, 2 * rows, wide), BF16),
            pltpu.VMEM((packed, 2 * rows), BF16),
            pltpu.VMEM((CHUNKS, 2 * rows, packed // CHUNKS), BF16),
            pltpu.VMEM((CHUNKS, 2 * rows, packed // CHUNKS), BF16),
            pltpu.VMEM((TP,) + across_peers, BF16),
            pltpu.VMEM((TP,) + across_peers, BF16),
            pltpu.VMEM((packed, 4 * units), F32),
            pltpu.VMEM((rows, 2 * units), F32),
            pltpu.VMEM((packed, 2 * units), BF16),
            pltpu.VMEM((3, 2 * rows, wide), BF16),
            pltpu.VMEM((2 * rows, wide), F32),
            pltpu.VMEM((2 * rows, wide), BF16),
            pltpu.VMEM((2 * rows, wide), BF16),
            pltpu.VMEM((2 * rows, wide), BF16),
            pltpu.VMEM(across_peers, BF16),
            pltpu.VMEM(across_peers, BF16),
            pltpu.VMEM(across_peers, BF16),
            pltpu.VMEM(across_peers, BF16),
            dma((5,)),
            dma((6,)),
            dma((6,)),
            dma((TP,)),
            dma((TP, CHUNKS)),
            dma((TP,)),
            dma((6,)),
            dma((6,)),
            dma((12,)),
            dma((12,)),
            dma((1,)),
            dma((CHUNKS,)),
            dma((1,)),
        ],
        compiler_params=pltpu.CompilerParams(
            collective_id=0, has_side_effects=True, vmem_limit_bytes=62 << 20
        ),
        cost_estimate=pl.CostEstimate(
            flops=2 * 5 * rows * quarter * 4 * units * 3 // 2,
            bytes_accessed=6 * quarter * 4 * units * 2,
            transcendentals=0,
        ),
    )(
        routes.T,
        route_weights.T,
        placement.reshape(1, window),
        lengths,
        hidden_in,
        shared_gate.reshape(pieces, wide, units),
        shared_up.reshape(pieces, wide, units),
        shared_down,
        expert_gate.reshape(pieces, wide, units),
        expert_up.reshape(pieces, wide, units),
        expert_down[0],
    )


def solution(mesh):
    in_specs = (
        P("dp", "tp"),
        P("dp"),
        P("dp", None),
        P("dp", None),
        P(),
        P(None, "tp"),
        P(None, "tp"),
        P("tp", None),
        P("dp", None, "tp"),
        P("dp", None, "tp"),
        P("dp", "tp", None),
    )
    out_specs = P("dp", "tp")
    return jax.shard_map(local, mesh=mesh, in_specs=in_specs, out_specs=out_specs, check_vma=False)
```

time: 153 us -> 145 us (0.948)
  local copies, waits for them, and re-layouts: 6.47 us -> 2.16 us
  Pallas kernels: 145 us -> 142 us
    pallas_call x1, Pallas kernels: 145 us -> 142 us  [local(): pl.pallas_call(functools.partial(kernel, groups), out_shape=jax.ShapeDtyp...]
    unnamed x3 -> x1, local copies, waits for them, and re-layouts: 5.14 us -> 2.16 us
where the time goes in v3:
time: 145 us
  Pallas kernels  142 us (98%)
  local copies, waits for them, and re-layouts  2.16 us (1%)
    pallas_call x1, Pallas kernels, local(): pl.pallas_call(functools.partial(kernel, groups), out_shape=jax.ShapeDtyp...  142 us

profile of v3, /device:TPU:1, one launch (start us, length us, event | category | flops | bytes accessed | tf_op | source)
XLA Modules:
  0.0 144.5 jit_solution(7302672201006675284)
XLA Ops:
  0.7 141.7 %shard_map.109 = bf16[256,1792]{1,0:T(8,128)(2,1)} custom-call(s32[8,256]{1,0:T(8,128)} %bitcast.13, f32[8,256]{1,0:T(8,128)} %bitcast.14, s32[1,32]{1,0:T(1,128)} %bitcast.15, s32[1]{0:T(128)S(6)} %copy.13.length_ref, bf16[256,1792]{1,0:T(8,128)(2,1)} %hidden_ref.1, bf16[8,896,256]{2,1,0:T(8,128)(2,1)} %bitcast.8, bf16[8,896,256]{2,1,0:T(8,128)(2,1)} %bitcast.9, ...), custom_call_target="tpu_custom_call" | custom-call | flops 7046430720 | bytes 22020096 | tf_op jit(solution)/shard_map/pallas_call | solution.py:502
  142.4 2.2 %copy.14 = bf16[256,1792]{1,0:T(8,128)(2,1)} copy(bf16[256,1792]{1,0:T(8,128)(2,1)} %shard_map.109) | data formatting | bytes 1835008

commit v4 on v3

--- a/solution.py
+++ b/solution.py
@@ -1,4 +1,5 @@
 import functools
+import math
 
 import jax
 import jax.numpy as jnp
@@ -12,7 +13,7 @@
 BF16 = jnp.bfloat16
 F32 = jnp.float32
 TP = 4
-CHUNKS = 4
+WINDOW = 4
 
 
 def dot(a, b):
@@ -29,6 +30,20 @@
     place = at - group * (2 * MOST_R)
     half = (place >= MOST_R).astype(jnp.int32)
     return group, half, place - MOST_R * half
+
+
+def side_of(groups):
+    side = math.isqrt(groups // 2)
+    assert 2 * side * side == groups and side & (side - 1) == 0
+    return side
+
+
+def device_at(place, side):
+    bits = side.bit_length() - 1
+    chunk = place >> (bits + 1)
+    x = (place >> 1) & (side - 1)
+    z = (chunk + side - x) & (side - 1)
+    return 2 * (side * x + z) + (place & 1)
 
 
 def kernel(
@@ -58,11 +73,9 @@
     acc,
     shared_acc,
     hid2,
-    s_part,
+    s_hidden,
     s_own,
-    s_relay,
-    s_left,
-    s_right,
+    others,
     e_relay,
     e_left,
     e_right,
@@ -75,6 +88,7 @@
     d_loc,
     s_send,
     s_recv,
+    p_sem,
     e_send,
     e_recv,
     c_send,
@@ -89,8 +103,9 @@
     rows = held.shape[1] // 2
     wide = held.shape[2]
     window = placement_ref.shape[1]
+    chunks = side_of(groups)
     hidden_units = ed_ref.shape[0]
-    per_chunk = groups // CHUNKS
+    per_chunk = groups // chunks
     chunk_rows = per_chunk * 2 * MOST_R
     packed = groups * 2 * MOST_R
     top = routes_ref.shape[0]
@@ -114,13 +129,19 @@
                 both.at[:, :, pl.ds(part * hidden_units, hidden_units)],
                 w_sem.at[1 + at],
             ).start()
-    for at, (down, kept) in enumerate(((sd_ref, wsd), (ed_ref, wed))):
-        for piece in range(2 * TP):
-            pltpu.make_async_copy(
-                down.at[:, pl.ds(piece * wide, wide)],
-                kept.at[piece // 2, pl.ds((piece % 2) * hidden_units, hidden_units)],
-                w_sem.at[3 + at],
-            ).start()
+    def columns(piece):
+        return pl.ds(pl.multiple_of(piece * wide, wide), wide)
+
+    for half in range(2):
+        pltpu.make_async_copy(
+            sd_ref.at[:, columns(2 * tp + half)], wsd.at[half], w_sem.at[3]
+        ).start()
+    for piece in range(2 * TP):
+        pltpu.make_async_copy(
+            ed_ref.at[:, pl.ds(piece * wide, wide)],
+            wed.at[piece // 2, pl.ds((piece % 2) * hidden_units, hidden_units)],
+            w_sem.at[4],
+        ).start()
 
     def arrived_weights(ref, at):
         pltpu.make_async_copy(ref, ref, w_sem.at[at]).wait()
@@ -136,7 +157,7 @@
             device_id_type=MESH,
         )
 
-    for neighbour in (left, right):
+    for neighbour in (left, right, across):
         pl.semaphore_signal(barrier, inc=1, device_id=(dp, neighbour), device_id_type=MESH)
 
     length = length_ref[0]
@@ -157,7 +178,7 @@
     ).astype(BF16)
     place = jnp.where(named > 0.0, dot(named.astype(BF16), before), -1.0)
     group_of, _, _ = slot_parts((packed, window), 0)
-    spread = jnp.where(placement_ref[...] == group_of, 1.0, 0.0).astype(BF16)
+    spread = jnp.where(placement_ref[...] == device_at(group_of, chunks), 1.0, 0.0).astype(BF16)
     _, half_of, want = slot_parts((packed, rows), 0)
     hit = dot(spread, place.astype(BF16)) == want.astype(F32)
     for half in range(2):
@@ -165,7 +186,7 @@
             hit, jnp.where(half_of == half, 1.0, 0.0), 0.0
         ).astype(BF16)
 
-    pl.semaphore_wait(barrier, groups - 1 + 2)
+    pl.semaphore_wait(barrier, groups - 1 + 3)
 
     def to(src, dst, send, recv, device):
         return pltpu.make_async_remote_copy(
@@ -205,55 +226,92 @@
     for at in range(2):
         gathers[at].start()
 
-    my_chunk = dp // per_chunk
+    chips = groups // 2
+    chip, core = dp // 2, lax.rem(dp, 2)
+    share = others.shape[3]
+
+    fetches = [
+        to(
+            sd_ref.at[pl.ds(pl.multiple_of(chip * share, share), share), columns(2 * device + core)],
+            others.at[core, chip, place],
+            s_send.at[at],
+            s_recv.at[at],
+            (dp, device),
+        )
+        for at, (device, place) in enumerate(((right, 2), (left, 0), (across, 1)))
+    ]
+    for copy in fetches:
+        copy.start()
+
+    my_x = dp // per_chunk
+    my_chunk = lax.rem(my_x + lax.rem(dp // 2, chunks), chunks)
+    my_place_in = 2 * my_x + lax.rem(dp, 2)
+    me = my_chunk * per_chunk + my_place_in
+
+    def rows_of(chunk):
+        return pl.ds(pl.multiple_of(chunk * chunk_rows, chunk_rows), chunk_rows)
 
     def chunk_at(k):
-        return lax.rem(my_chunk + k, CHUNKS)
+        return lax.rem(my_chunk + k, chunks)
 
     def send_chunk(source, landing, chunk, send, recv, local):
         @pl.loop(0, per_chunk)
         def _(step):
-            target = chunk * per_chunk + lax.rem(dp + step, per_chunk)
-
-            @pl.when(target != dp)
+            place = lax.rem(my_place_in + step, per_chunk)
+            x = place // 2
+            device = 2 * (chunks * x + lax.rem(chunk + chunks - x, chunks)) + lax.rem(place, 2)
+            there = chunk * per_chunk + place
+
+            @pl.when(device != dp)
             def _():
-                to(source.at[target], landing.at[dp], send, recv, (target, tp)).start()
-
-            @pl.when(target == dp)
+                to(source.at[there], landing.at[me], send, recv, (device, tp)).start()
+
+            @pl.when(device == dp)
             def _():
-                pltpu.make_async_copy(source.at[dp], landing.at[dp], local).start()
+                pltpu.make_async_copy(source.at[me], landing.at[me], local).start()
 
     def wait_peers(ref, sem, number):
         view = ref.at[pl.ds(0, number)]
         pltpu.make_async_copy(view, view, sem).wait()
 
     def from_chunk(k):
-        return lax.rem(my_chunk + CHUNKS - k, CHUNKS)
+        return lax.rem(my_chunk + chunks - k, chunks)
 
     def wait_chunk(ref, k, recv, local):
         wait_peers(ref, recv.at[k], per_chunk - 1 if k == 0 else per_chunk)
         if k == 0:
             wait_peers(ref, local, 1)
 
+    def issue(slot, k):
+        send_chunk(
+            outgoing.at[slot],
+            arrived.at[slot],
+            chunk_at(k),
+            d_send.at[slot, k],
+            d_recv.at[slot, k],
+            d_loc.at[slot],
+        )
+
+    def wait_issued(slot, k):
+        wait_peers(outgoing.at[slot], d_send.at[slot, k], per_chunk - (k == 0))
+
+    def issue_next(slot, *ks):
+        for k in ks:
+            earlier = slot * chunks + k - WINDOW
+            if earlier >= 0:
+                wait_issued(earlier // chunks, earlier % chunks)
+            issue(slot, k)
+
     def select(slot):
-        @pl.loop(0, CHUNKS)
+        @pl.loop(0, chunks)
         def _(k):
             chunk = chunk_at(k)
-            picked = dot(
-                sel[pl.ds(pl.multiple_of(chunk * chunk_rows, chunk_rows), chunk_rows), :],
-                held[slot],
-            )
+            picked = dot(sel[rows_of(chunk), :], held[slot])
             outgoing[slot, pl.ds(chunk * per_chunk, per_chunk)] = picked.reshape(
                 per_chunk, 2 * MOST_R, wide
             ).astype(BF16)
-            send_chunk(
-                outgoing.at[slot],
-                arrived.at[slot],
-                chunk,
-                d_send.at[slot],
-                d_recv.at[slot, k],
-                d_loc.at[slot],
-            )
+            if slot == 0:
+                issue(slot, k)
 
     def shared_step(slot):
         first, second = pieces[slot]
@@ -267,9 +325,6 @@
 
     def load_chunk(ref, k):
         return ref[pl.ds(k * per_chunk, per_chunk)].astype(F32).reshape(chunk_rows, wide)
-
-    def rows_of(chunk):
-        return pl.ds(pl.multiple_of(chunk * chunk_rows, chunk_rows), chunk_rows)
 
     select(0)
     arrived_weights(wsgu, 1)
@@ -282,9 +337,9 @@
     placement_col = jnp.transpose(
         jnp.broadcast_to(placement_ref[...].astype(F32), (8, window))
     )[:, :1]
-    for chunk in range(CHUNKS):
+    for chunk in range(chunks):
         group_of, _, _ = slot_parts((window, chunk_rows), 1)
-        group_of = (group_of + chunk * per_chunk).astype(F32)
+        group_of = device_at(group_of + chunk * per_chunk, chunks).astype(F32)
         spread = jnp.where(placement_col == group_of, 1.0, 0.0).astype(BF16)
         _, half_of, want = slot_parts((rows, chunk_rows), 1)
         hit = dot(place, spread) == want.astype(F32)
@@ -294,52 +349,6 @@
                 kept[chunk, pl.ds(half * rows, rows), :] = jnp.where(
                     half_of == half, value, 0.0
                 ).astype(BF16)
-
-    for at in (0, 1):
-        gathers[at].wait_recv()
-        gathers[at + 2].start()
-        gathers[at + 4].start()
-    select(1)
-    shared_step(1)
-    for slot in (2, 3):
-        for at in (0, 1):
-            gathers[2 * slot - 2 + at].wait_recv()
-        select(slot)
-        shared_step(slot)
-
-    shared_hidden = (
-        silu(shared_acc[:, pl.ds(0, hidden_units)])
-        * shared_acc[:, pl.ds(hidden_units, hidden_units)]
-    ).astype(BF16)
-    arrived_weights(wsd, 3)
-    for at, owner in ((0, across), (1, right), (2, left), (3, tp)):
-        for half in range(2):
-            part = dot(shared_hidden, wsd[owner, pl.ds(half * hidden_units, hidden_units)])
-            if at < 3:
-                s_part[at, pl.ds(half * rows, rows)] = part.astype(BF16)
-            else:
-                s_own[pl.ds(half * rows, rows)] = part
-
-    def s_copy(at, part, half, landing, device):
-        where = pl.ds(half * rows, rows)
-        return to(
-            s_part.at[part, where],
-            landing.at[where],
-            s_send.at[at],
-            s_recv.at[at],
-            (dp, device),
-        )
-
-    shared_sends = [
-        s_copy(0, 0, 0, s_relay, right),
-        s_copy(1, 0, 1, s_relay, left),
-        s_copy(2, 1, 1, s_left, right),
-        s_copy(3, 2, 0, s_right, left),
-        s_copy(4, 1, 0, s_left, right),
-        s_copy(5, 2, 1, s_right, left),
-    ]
-    for at in range(2):
-        shared_sends[at].start()
 
     both = 2 * hidden_units
 
@@ -389,7 +398,7 @@
         )
 
     relays, directs, passed = [], [], []
-    for k in range(CHUNKS):
+    for k in range(chunks):
         ahead, behind = ((1, right, e_left), (2, left, e_right))[:: 1 if k % 2 == 0 else -1]
         relays.append(e_copy(k, 0, k, e_relay, ahead[1]))
         directs.append(e_copy(4 + k, behind[0], k, behind[2], behind[1]))
@@ -406,7 +415,6 @@
 
     def finish(k):
         chunk = from_chunk(k)
-        down(None, tp, k)
         directs[k].wait_recv()
         passed[k][1].wait_recv()
         total = (
@@ -419,46 +427,121 @@
         ).astype(BF16)
         send_chunk(outgoing.at[3], came, chunk, c_send.at[0], c_recv.at[k], c_loc.at[0])
 
+    first, second = range(chunks // 2), range(chunks // 2, chunks)
+    for at in (0, 1):
+        gathers[at].wait_recv()
+        gathers[at + 2].start()
+        gathers[at + 4].start()
+    select(1)
+    for k in range(chunks - WINDOW):
+        wait_issued(0, k)
+    issue_next(1, *first)
     arrived_weights(wgu, 2)
-    for k in range(CHUNKS):
+    for k in range(chunks):
         expert_chunk(0, k)
+    issue_next(1, *second)
+    shared_step(1)
+    for k in first:
+        expert_chunk(1, k)
     for at in (2, 3):
-        shared_sends[at].start()
-    for k in range(CHUNKS):
+        gathers[at].wait_recv()
+    select(2)
+    issue_next(2, *first)
+    for at in (4, 5):
+        gathers[at].wait_recv()
+    select(3)
+    shared_step(2)
+    shared_step(3)
+
+    shared_hidden = (
+        silu(shared_acc[:, pl.ds(0, hidden_units)])
+        * shared_acc[:, pl.ds(hidden_units, hidden_units)]
+    ).astype(BF16)
+    s_hidden[0] = shared_hidden
+    hidden_sends = [
+        to(
+            s_hidden.at[0],
+            s_hidden.at[place],
+            s_send.at[3 + at],
+            s_recv.at[3 + at],
+            (dp, device),
+        )
+        for at, (device, place) in enumerate(((right, 3), (left, 1), (across, 2)))
+    ]
+    for copy in hidden_sends:
+        copy.start()
+
+    issue_next(2, *second)
+    for k in second:
         expert_chunk(1, k)
-    for at, part, half in ((0, 1, 0), (1, 2, 1)):
-        shared_sends[at].wait_recv()
-        where = pl.ds(half * rows, rows)
-        s_part[part, where] = (
-            s_part[part, where].astype(F32) + s_relay[where].astype(F32)
-        ).astype(BF16)
-        shared_sends[at + 4].start()
-    for k in range(CHUNKS):
+    issue_next(3, *first)
+    for k in first:
+        expert_chunk(2, k)
+    issue_next(3, *second)
+
+    for copy in fetches:
+        copy.wait_recv()
+
+    @pl.loop(1, chips)
+    def _(step):
+        target = 2 * lax.rem(chip + step, chips) + core
+        to(
+            others.at[core, chip],
+            others.at[core, chip],
+            p_sem.at[0],
+            p_sem.at[1],
+            (target, tp),
+        ).start()
+
+    for k in second:
         expert_chunk(2, k)
     arrived_weights(wed, 4)
-    for slot in range(3):
-        wait_peers(outgoing.at[slot], d_send.at[slot], groups - 1)
-    for k in range(CHUNKS):
+    for k in range(chunks):
         expert_chunk(3, k)
         activate(from_chunk(k))
         down(0, across, k)
-        relays[k].start()
+        if k in first:
+            relays[k].start()
         slot, device = ((2, left), (1, right))[k % 2]
         down(slot, device, k)
-        directs[k].start()
+        if k in first:
+            directs[k].start()
         (slot, device, _), _ = passed[k]
         down(slot, device, k)
-        if k:
-            pass_on(k - 1)
-    pass_on(CHUNKS - 1)
-    for at in range(2, 6):
-        shared_sends[at].wait_recv()
-    s_own[...] = s_own[...] + s_left[...].astype(F32) + s_right[...].astype(F32)
-    wait_peers(outgoing.at[3], d_send.at[3], groups - 1)
-    for k in range(CHUNKS):
+        down(None, tp, k)
+    for k in first:
+        pass_on(k)
+    for k in second:
+        relays[k].start()
+    for at in range(WINDOW):
+        wait_issued(3, chunks - 1 - at)
+    for k in first:
         finish(k)
-
-    for k in range(CHUNKS):
+    for k in second:
+        directs[k].start()
+    for k in second:
+        pass_on(k)
+    wait_peers(others.at[core], p_sem.at[1], chips - 1)
+    swap = to(
+        others.at[core], others.at[core], p_sem.at[2], p_sem.at[3], (dp + 1 - 2 * core, tp)
+    )
+    swap.start()
+    for k in second:
+        finish(k)
+
+    for copy in hidden_sends:
+        copy.wait_recv()
+    arrived_weights(wsd, 3)
+    swap.wait_recv()
+    for half in range(2):
+        total = dot(s_hidden[0], wsd[half])
+        for place in range(TP - 1):
+            total += dot(
+                s_hidden[place + 1], others[half, :, place].reshape(hidden_units, wide)
+            )
+        s_own[pl.ds(half * rows, rows)] = total
+
+    for k in range(chunks):
         wait_chunk(came, k, c_recv, c_loc.at[0])
         chunk = chunk_at(k)
         block = load_chunk(came, chunk).astype(BF16)
@@ -469,8 +552,10 @@
             keep, s_own[pl.ds(half * rows, rows)], 0.0
         ).astype(out_ref.dtype)
 
-    for copy in gathers + shared_sends + relays + directs + [copy for _, copy in passed]:
+    sends = gathers + fetches + hidden_sends + [swap]
+    for copy in sends + relays + directs + [copy for _, copy in passed]:
         copy.wait_send()
+    wait_peers(others.at[core], p_sem.at[0], chips - 1)
     wait_peers(outgoing.at[3], c_send.at[0], groups - 1)
 
 
@@ -493,6 +578,7 @@
     pieces = 2 * TP
     units = shared_gate.shape[1]
     window = placement.shape[0]
+    chunks = side_of(groups)
     packed = groups * 2 * MOST_R
     across_peers = (groups, 2 * MOST_R, wide)
     vmem = pl.BlockSpec(memory_space=pltpu.VMEM)
@@ -506,23 +592,21 @@
         out_specs=vmem,
         scratch_shapes=[
             pltpu.VMEM((pieces, wide, 2 * units), BF16),
-            pltpu.VMEM((TP, 2 * units, wide), BF16),
+            pltpu.VMEM((2, units, wide), BF16),
             pltpu.VMEM((pieces, wide, 2 * units), BF16),
             pltpu.VMEM((TP, 2 * units, wide), BF16),
             pltpu.VMEM((TP, 2 * rows, wide), BF16),
             pltpu.VMEM((packed, 2 * rows), BF16),
-            pltpu.VMEM((CHUNKS, 2 * rows, packed // CHUNKS), BF16),
-            pltpu.VMEM((CHUNKS, 2 * rows, packed // CHUNKS), BF16),
+            pltpu.VMEM((chunks, 2 * rows, packed // chunks), BF16),
+            pltpu.VMEM((chunks, 2 * rows, packed // chunks), BF16),
             pltpu.VMEM((TP,) + across_peers, BF16),
             pltpu.VMEM((TP,) + across_peers, BF16),
             pltpu.VMEM((packed, 4 * units), F32),
             pltpu.VMEM((rows, 2 * units), F32),
             pltpu.VMEM((packed, 2 * units), BF16),
-            pltpu.VMEM((3, 2 * rows, wide), BF16),
+            pltpu.VMEM((TP, rows, units), BF16),
             pltpu.VMEM((2 * rows, wide), F32),
-            pltpu.VMEM((2 * rows, wide), BF16),
-            pltpu.VMEM((2 * rows, wide), BF16),
-            pltpu.VMEM((2 * rows, wide), BF16),
+            pltpu.VMEM((2, groups // 2, TP - 1, 2 * units // groups, wide), BF16),
             pltpu.VMEM(across_peers, BF16),
             pltpu.VMEM(across_peers, BF16),
             pltpu.VMEM(across_peers, BF16),
@@ -530,15 +614,16 @@
             dma((5,)),
             dma((6,)),
             dma((6,)),
-            dma((TP,)),
-            dma((TP, CHUNKS)),
+            dma((TP, chunks)),
+            dma((TP, chunks)),
             dma((TP,)),
             dma((6,)),
             dma((6,)),
+            dma((4,)),
             dma((12,)),
             dma((12,)),
             dma((1,)),
-            dma((CHUNKS,)),
+            dma((chunks,)),
             dma((1,)),
         ],
         compiler_params=pltpu.CompilerParams(

time: 145 us -> 135 us (0.931)
  Pallas kernels: 142 us -> 131 us
    pallas_call x1, Pallas kernels: 142 us -> 131 us  [local(): pl.pallas_call(functools.partial(kernel, groups), out_shape=jax.ShapeDtyp...]
where the time goes in v4:
time: 135 us; the launch traced here: 134 us
  Pallas kernels  131 us (97%)
  local copies, waits for them, and re-layouts  2.16 us (2%)
    pallas_call x1, Pallas kernels, local(): pl.pallas_call(functools.partial(kernel, groups), out_shape=jax.ShapeDtyp...  131 us

profile of v4, /device:TPU:1, one launch (start us, length us, event | category | flops | bytes accessed | tf_op | source)
XLA Modules:
  0.0 133.5 jit_solution(10802674935632967119)
XLA Ops:
  0.7 130.7 %shard_map.109 = bf16[256,1792]{1,0:T(8,128)(2,1)} custom-call(s32[8,256]{1,0:T(8,128)} %bitcast.13, f32[8,256]{1,0:T(8,128)} %bitcast.14, s32[1,32]{1,0:T(1,128)} %bitcast.15, s32[1]{0:T(128)S(6)} %copy.13.length_ref, bf16[256,1792]{1,0:T(8,128)(2,1)} %hidden_ref.1, bf16[8,896,256]{2,1,0:T(8,128)(2,1)} %bitcast.8, bf16[8,896,256]{2,1,0:T(8,128)(2,1)} %bitcast.9, ...), custom_call_target="tpu_custom_call" | custom-call | flops 7046430720 | bytes 22020096 | tf_op jit(solution)/shard_map/pallas_call | solution.py:588
  131.4 2.2 %copy.14 = bf16[256,1792]{1,0:T(8,128)(2,1)} copy(bf16[256,1792]{1,0:T(8,128)(2,1)} %shard_map.109) | data formatting | bytes 1835008

commit v5 on v4

--- a/solution.py
+++ b/solution.py
@@ -76,6 +76,7 @@
     s_hidden,
     s_own,
     others,
+    for_left,
     e_relay,
     e_left,
     e_right,
@@ -295,12 +296,19 @@
     def wait_issued(slot, k):
         wait_peers(outgoing.at[slot], d_send.at[slot, k], per_chunk - (k == 0))
 
-    def issue_next(slot, *ks):
-        for k in ks:
-            earlier = slot * chunks + k - WINDOW
-            if earlier >= 0:
-                wait_issued(earlier // chunks, earlier % chunks)
+    queue = [(0, k) for k in range(chunks)]
+    waited = []
+
+    def wait_queue(number):
+        while len(waited) < number:
+            wait_issued(*queue[len(waited)])
+            waited.append(1)
+
+    def issue_next(*which):
+        for slot, k in which:
+            wait_queue(len(queue) + 1 - WINDOW)
             issue(slot, k)
+            queue.append((slot, k))
 
     def select(slot):
         @pl.loop(0, chunks)
@@ -377,11 +385,13 @@
             half_of == 1, pltpu.roll(inner, MOST_R, 0), 0.0
         ).astype(BF16)
 
+    partial = (outgoing.at[0], outgoing.at[1], for_left)
+
     def down(slot, owner, k):
         chunk = from_chunk(k)
         part = dot(hid2[rows_of(chunk), :], wed[owner])
         if slot is not None:
-            outgoing[slot, pl.ds(chunk * per_chunk, per_chunk)] = part.reshape(
+            partial[slot][pl.ds(chunk * per_chunk, per_chunk)] = part.reshape(
                 per_chunk, 2 * MOST_R, wide
             ).astype(BF16)
         else:
@@ -390,7 +400,7 @@
     def e_copy(at, slot, k, landing, device):
         where = pl.ds(from_chunk(k) * per_chunk, per_chunk)
         return to(
-            outgoing.at[slot, where],
+            partial[slot].at[where],
             landing.at[where],
             e_send.at[at],
             e_recv.at[at],
@@ -408,8 +418,8 @@
         (slot, _, _), copy = passed[k]
         where = pl.ds(from_chunk(k) * per_chunk, per_chunk)
         relays[k].wait_recv()
-        outgoing[slot, where] = (
-            outgoing[slot, where].astype(F32) + e_relay[where].astype(F32)
+        partial[slot][where] = (
+            partial[slot][where].astype(F32) + e_relay[where].astype(F32)
         ).astype(BF16)
         copy.start()
 
@@ -422,10 +432,10 @@
             + load_chunk(e_left, chunk)
             + load_chunk(e_right, chunk)
         )
-        outgoing[3, pl.ds(chunk * per_chunk, per_chunk)] = total.reshape(
+        outgoing[2, pl.ds(chunk * per_chunk, per_chunk)] = total.reshape(
             per_chunk, 2 * MOST_R, wide
         ).astype(BF16)
-        send_chunk(outgoing.at[3], came, chunk, c_send.at[0], c_recv.at[k], c_loc.at[0])
+        send_chunk(outgoing.at[2], came, chunk, c_send.at[0], c_recv.at[k], c_loc.at[0])
 
     first, second = range(chunks // 2), range(chunks // 2, chunks)
     for at in (0, 1):
@@ -433,23 +443,21 @@
         gathers[at + 2].start()
         gathers[at + 4].start()
     select(1)
-    for k in range(chunks - WINDOW):
-        wait_issued(0, k)
-    issue_next(1, *first)
+    issue_next(*((1, k) for k in first))
     arrived_weights(wgu, 2)
     for k in range(chunks):
         expert_chunk(0, k)
-    issue_next(1, *second)
+    issue_next(*((1, k) for k in second))
     shared_step(1)
     for k in first:
         expert_chunk(1, k)
     for at in (2, 3):
         gathers[at].wait_recv()
     select(2)
-    issue_next(2, *first)
     for at in (4, 5):
         gathers[at].wait_recv()
     select(3)
+    issue_next((2, 0), (3, 0))
     shared_step(2)
     shared_step(3)
 
@@ -471,13 +479,31 @@
     for copy in hidden_sends:
         copy.start()
 
-    issue_next(2, *second)
     for k in second:
         expert_chunk(1, k)
-    issue_next(3, *first)
-    for k in first:
+    arrived_weights(wed, 4)
+
+    def last_steps(k):
         expert_chunk(2, k)
-    issue_next(3, *second)
+        expert_chunk(3, k)
+        activate(from_chunk(k))
+        down(0, across, k)
+        relays[k].start()
+        slot, device = ((2, left), (1, right))[k % 2]
+        down(slot, device, k)
+        if k < chunks - 1:
+            directs[k].start()
+        (slot, device, _), _ = passed[k]
+        down(slot, device, k)
+        down(None, tp, k)
+
+    for k in range(chunks):
+        if k + 1 < chunks:
+            issue_next((2, k + 1), (3, k + 1))
+        last_steps(k)
+        if k >= 1:
+            pass_on(k - 1)
+    wait_queue(len(queue))
 
     for copy in fetches:
         copy.wait_recv()
@@ -493,41 +519,18 @@
             (target, tp),
         ).start()
 
-    for k in second:
-        expert_chunk(2, k)
-    arrived_weights(wed, 4)
-    for k in range(chunks):
-        expert_chunk(3, k)
-        activate(from_chunk(k))
-        down(0, across, k)
-        if k in first:
-            relays[k].start()
-        slot, device = ((2, left), (1, right))[k % 2]
-        down(slot, device, k)
-        if k in first:
-            directs[k].start()
-        (slot, device, _), _ = passed[k]
-        down(slot, device, k)
-        down(None, tp, k)
-    for k in first:
-        pass_on(k)
-    for k in second:
-        relays[k].start()
-    for at in range(WINDOW):
-        wait_issued(3, chunks - 1 - at)
-    for k in first:
+    for k in range(chunks - 2):
         finish(k)
-    for k in second:
-        directs[k].start()
-    for k in second:
-        pass_on(k)
+    passed[chunks - 2][1].wait_send()
+    directs[chunks - 1].start()
+    pass_on(chunks - 1)
+    finish(chunks - 2)
     wait_peers(others.at[core], p_sem.at[1], chips - 1)
     swap = to(
         others.at[core], others.at[core], p_sem.at[2], p_sem.at[3], (dp + 1 - 2 * core, tp)
     )
     swap.start()
-    for k in second:
-        finish(k)
+    finish(chunks - 1)
 
     for copy in hidden_sends:
         copy.wait_recv()
@@ -553,10 +556,10 @@
         ).astype(out_ref.dtype)
 
     sends = gathers + fetches + hidden_sends + [swap]
-    for copy in sends + relays + directs + [copy for _, copy in passed]:
+    for copy in sends + relays + directs + [copy for k, (_, copy) in enumerate(passed) if k != chunks - 2]:
         copy.wait_send()
     wait_peers(others.at[core], p_sem.at[0], chips - 1)
-    wait_peers(outgoing.at[3], c_send.at[0], groups - 1)
+    wait_peers(outgoing.at[2], c_send.at[0], groups - 1)
 
 
 def local(
@@ -611,6 +614,7 @@
             pltpu.VMEM(across_peers, BF16),
             pltpu.VMEM(across_peers, BF16),
             pltpu.VMEM(across_peers, BF16),
+            pltpu.VMEM(across_peers, BF16),
             dma((5,)),
             dma((6,)),
             dma((6,)),

time: 135 us -> 132 us (0.978)
  Pallas kernels: 131 us -> 129 us
    pallas_call x1, Pallas kernels: 131 us -> 129 us  [local(): pl.pallas_call(functools.partial(kernel, groups), out_shape=jax.ShapeDtyp...]
where the time goes in v5:
time: 132 us
  Pallas kernels  129 us (98%)
  local copies, waits for them, and re-layouts  2.16 us (2%)
    pallas_call x1, Pallas kernels, local(): pl.pallas_call(functools.partial(kernel, groups), out_shape=jax.ShapeDtyp...  129 us

profile of v5, /device:TPU:1, one launch (start us, length us, event | category | flops | bytes accessed | tf_op | source)
XLA Modules:
  0.0 131.6 jit_solution(17795916400944571170)
XLA Ops:
  0.7 128.8 %shard_map.109 = bf16[256,1792]{1,0:T(8,128)(2,1)} custom-call(s32[8,256]{1,0:T(8,128)} %bitcast.13, f32[8,256]{1,0:T(8,128)} %bitcast.14, s32[1,32]{1,0:T(1,128)} %bitcast.15, s32[1]{0:T(128)S(6)} %copy.13.length_ref, bf16[256,1792]{1,0:T(8,128)(2,1)} %hidden_ref.1, bf16[8,896,256]{2,1,0:T(8,128)(2,1)} %bitcast.8, bf16[8,896,256]{2,1,0:T(8,128)(2,1)} %bitcast.9, ...), custom_call_target="tpu_custom_call" | custom-call | flops 7046430720 | bytes 22020096 | tf_op jit(solution)/shard_map/pallas_call | solution.py:591
  129.4 2.2 %copy.14 = bf16[256,1792]{1,0:T(8,128)(2,1)} copy(bf16[256,1792]{1,0:T(8,128)(2,1)} %shard_map.109) | data formatting | bytes 1835008

commit v6 on v5

--- a/solution.py
+++ b/solution.py
@@ -228,13 +228,23 @@
         gathers[at].start()
 
     chips = groups // 2
-    chip, core = dp // 2, lax.rem(dp, 2)
+    core = lax.rem(dp, 2)
+    chip_x, chip_z = dp // (2 * chunks), lax.rem(dp // 2, chunks)
+    near = core * chip_x + (1 - core) * chip_z
+    far = core * chip_z + (1 - core) * chip_x
+    mine = far * chunks + near
+
+    def spread_to(near_at, far_at):
+        x = core * near_at + (1 - core) * far_at
+        z = core * far_at + (1 - core) * near_at
+        return (2 * (x * chunks + z) + core, tp)
+
     share = others.shape[3]
 
     fetches = [
         to(
-            sd_ref.at[pl.ds(pl.multiple_of(chip * share, share), share), columns(2 * device + core)],
-            others.at[core, chip, place],
+            sd_ref.at[pl.ds(pl.multiple_of(mine * share, share), share), columns(2 * device + core)],
+            others.at[core, mine, place],
             s_send.at[at],
             s_recv.at[at],
             (dp, device),
@@ -454,6 +464,15 @@
     for at in (2, 3):
         gathers[at].wait_recv()
     select(2)
+    for copy in fetches:
+        copy.wait_recv()
+
+    @pl.loop(1, chunks)
+    def _(step):
+        piece = others.at[core, mine]
+        device = spread_to(lax.rem(near + step, chunks), far)
+        to(piece, piece, p_sem.at[0], p_sem.at[1], device).start()
+
     for at in (4, 5):
         gathers[at].wait_recv()
     select(3)
@@ -505,19 +524,13 @@
             pass_on(k - 1)
     wait_queue(len(queue))
 
-    for copy in fetches:
-        copy.wait_recv()
-
-    @pl.loop(1, chips)
+    wait_peers(others.at[core], p_sem.at[1], chunks - 1)
+
+    @pl.loop(1, chunks)
     def _(step):
-        target = 2 * lax.rem(chip + step, chips) + core
-        to(
-            others.at[core, chip],
-            others.at[core, chip],
-            p_sem.at[0],
-            p_sem.at[1],
-            (target, tp),
-        ).start()
+        line = others.at[core, pl.ds(far * chunks, chunks)]
+        device = spread_to(near, lax.rem(far + step, chunks))
+        to(line, line, p_sem.at[4], p_sem.at[5], device).start()
 
     for k in range(chunks - 2):
         finish(k)
@@ -525,7 +538,7 @@
     directs[chunks - 1].start()
     pass_on(chunks - 1)
     finish(chunks - 2)
-    wait_peers(others.at[core], p_sem.at[1], chips - 1)
+    wait_peers(others.at[core], p_sem.at[5], chips - chunks)
     swap = to(
         others.at[core], others.at[core], p_sem.at[2], p_sem.at[3], (dp + 1 - 2 * core, tp)
     )
@@ -558,7 +571,8 @@
     sends = gathers + fetches + hidden_sends + [swap]
     for copy in sends + relays + directs + [copy for k, (_, copy) in enumerate(passed) if k != chunks - 2]:
         copy.wait_send()
-    wait_peers(others.at[core], p_sem.at[0], chips - 1)
+    wait_peers(others.at[core], p_sem.at[0], chunks - 1)
+    wait_peers(others.at[core], p_sem.at[4], chips - chunks)
     wait_peers(outgoing.at[2], c_send.at[0], groups - 1)
 
 
@@ -623,7 +637,7 @@
             dma((TP,)),
             dma((6,)),
             dma((6,)),
-            dma((4,)),
+            dma((6,)),
             dma((12,)),
             dma((12,)),
             dma((1,)),

time: 132 us -> 125 us (0.947)
  the two profiles are of different devices: /device:TPU:1 before, /device:TPU:16 now
where the time goes in v6:
time: 125 us
  Pallas kernels  122 us (98%)
  local copies, waits for them, and re-layouts  2.16 us (2%)
    pallas_call x1, Pallas kernels, local(): pl.pallas_call(functools.partial(kernel, groups), out_shape=jax.ShapeDtyp...  122 us

profile of v6, /device:TPU:16, one launch (start us, length us, event | category | flops | bytes accessed | tf_op | source)
XLA Modules:
  0.0 125.3 jit_solution(10414170825469064537)
XLA Ops:
  0.7 122.5 %shard_map.109 = bf16[256,1792]{1,0:T(8,128)(2,1)} custom-call(s32[8,256]{1,0:T(8,128)} %bitcast.13, f32[8,256]{1,0:T(8,128)} %bitcast.14, s32[1,32]{1,0:T(1,128)} %bitcast.15, s32[1]{0:T(128)S(6)} %copy.13.length_ref, bf16[256,1792]{1,0:T(8,128)(2,1)} %hidden_ref.1, bf16[8,896,256]{2,1,0:T(8,128)(2,1)} %bitcast.8, bf16[8,896,256]{2,1,0:T(8,128)(2,1)} %bitcast.9, ...), custom_call_target="tpu_custom_call" | custom-call | flops 7046430720 | bytes 22020096 | tf_op jit(solution)/shard_map/pallas_call | solution.py:605
  123.1 2.2 %copy.14 = bf16[256,1792]{1,0:T(8,128)(2,1)} copy(bf16[256,1792]{1,0:T(8,128)(2,1)} %shard_map.109) | data formatting | bytes 1835008

commit v7 on v6

--- a/solution.py
+++ b/solution.py
@@ -524,6 +524,8 @@
             pass_on(k - 1)
     wait_queue(len(queue))
 
+    for k in range(chunks - 2):
+        finish(k)
     wait_peers(others.at[core], p_sem.at[1], chunks - 1)
 
     @pl.loop(1, chunks)
@@ -532,8 +534,6 @@
         device = spread_to(near, lax.rem(far + step, chunks))
         to(line, line, p_sem.at[4], p_sem.at[5], device).start()
 
-    for k in range(chunks - 2):
-        finish(k)
     passed[chunks - 2][1].wait_send()
     directs[chunks - 1].start()
     pass_on(chunks - 1)

time: 125 us -> 124 us (level)
  the two profiles are of different devices: /device:TPU:16 before, /device:TPU:1 now
where the time goes in v7:
time: 124 us
  Pallas kernels  121 us (98%)
  local copies, waits for them, and re-layouts  2.16 us (2%)
    pallas_call x1, Pallas kernels, local(): pl.pallas_call(functools.partial(kernel, groups), out_shape=jax.ShapeDtyp...  121 us

profile of v7, /device:TPU:1, one launch (start us, length us, event | category | flops | bytes accessed | tf_op | source)
XLA Modules:
  0.0 123.5 jit_solution(553093972134447667)
XLA Ops:
  0.7 120.7 %shard_map.109 = bf16[256,1792]{1,0:T(8,128)(2,1)} custom-call(s32[8,256]{1,0:T(8,128)} %bitcast.13, f32[8,256]{1,0:T(8,128)} %bitcast.14, s32[1,32]{1,0:T(1,128)} %bitcast.15, s32[1]{0:T(128)S(6)} %copy.13.length_ref, bf16[256,1792]{1,0:T(8,128)(2,1)} %hidden_ref.1, bf16[8,896,256]{2,1,0:T(8,128)(2,1)} %bitcast.8, bf16[8,896,256]{2,1,0:T(8,128)(2,1)} %bitcast.9, ...), custom_call_target="tpu_custom_call" | custom-call | flops 7046430720 | bytes 22020096 | tf_op jit(solution)/shard_map/pallas_call | solution.py:605
  121.4 2.2 %copy.14 = bf16[256,1792]{1,0:T(8,128)(2,1)} copy(bf16[256,1792]{1,0:T(8,128)(2,1)} %shard_map.109) | data formatting | bytes 1835008
